TPU v7x, 256 devices: a whole 4x4x8 slice. The times are simulated.
256 devices in a mesh: row: 8 (over y, x_hi), col: 32 (over z, x_lo, core).
Axes of the slice: x: 4 (x_hi: 2, x_lo: 2; x = x_hi * 2 + x_lo), y: 4, z: 8, core: 2. Of those that a mesh axis runs over, the one named last changes fastest.
Arguments:
- ancestor: float32 [2, 4096, 4096], P(None, 'row', 'col')
- panel: float32 [2, 4096, 512], P(None, 'col'), may hold values from -0.75 to 0.75
- factor_inv: float32 [2, 512, 512], P(None, 'row'), as said below
- pattern: int32 [2, 16], replicated, may hold values from 0 to 15, each once within a row
Outputs:
- column_block: float32 [2, 4096, 512], P(None, ('row', 'col'))
- diagonal_inv: float32 [2, 512], replicated
Inputs may be any that keep to these rules, and one draw needn't show every extreme that they name: `pattern`: each row names each of the 16 tile positions exactly once. `factor_inv`: each block is lower triangular with its diagonal between 0.5 and 2.
All inputs are finite; a program needn't handle non-finite values.
Results may differ from a plain program's by a relative error of at most 0.0001.
Values sent between devices are 32-bit elements; how exact they have to be, the bound alone decides.
A program may use at most 64 MiB of HBM per device.

v0:
```python
import jax
import jax.numpy as jnp
from jax import lax
from jax.sharding import PartitionSpec as P

B = 256


def scatter_rows(totals, targets, limit, pieces):
    inside = (targets >= 0) & (targets < limit)
    targets = jnp.where(inside, targets, limit)

    def one_group(accum, target, values):
        return accum.at[target].add(values, mode="drop")

    return jax.vmap(one_group)(totals, targets, pieces)


def spread_tiles(moving, pattern, row_first, col_first, row_count, col_count):
    groups = moving.shape[0]
    width_cols = moving.shape[2]
    initial = (
        jnp.zeros((groups, col_count, width_cols), jnp.float32),
        jnp.zeros((groups, row_count, width_cols), jnp.float32),
    )
    pieces = lax.all_gather(moving, "col", axis=1, tiled=True)
    count = pieces.shape[1]
    global_rows = jnp.arange(count, dtype=jnp.int32)
    ancestor_rows = jnp.take(pattern, global_rows // B, axis=1) * B + global_rows % B
    col_totals = scatter_rows(initial[0], ancestor_rows - col_first, col_count, pieces)
    row_totals = scatter_rows(initial[1], ancestor_rows - row_first, row_count, pieces)
    return (col_totals, row_totals)


def per_device(ancestor, panel, factor_inv, pattern):
    highest = lax.Precision.HIGHEST
    row_count = ancestor.shape[1]
    col_count = ancestor.shape[2]
    row_first = lax.axis_index("row") * row_count
    col_first = lax.axis_index("col") * col_count
    full_inverse = lax.all_gather(factor_inv, "row", axis=1, tiled=True)
    moving = jnp.einsum("srw,swv->srv", panel, full_inverse, precision=highest)
    col_part, row_part = spread_tiles(moving, pattern, row_first, col_first, row_count, col_count)
    partial_value = jnp.einsum("sij,sjw->siw", ancestor, col_part, precision=highest)
    summed = lax.psum_scatter(partial_value, "col", scatter_dimension=1, tiled=True)
    column_sq = jnp.sum(full_inverse * full_inverse, axis=1)
    local_terms = jnp.sum(row_part * partial_value, axis=1)
    totals = lax.psum(local_terms, ("row", "col"))
    column_block = -summed
    diagonal_inv = column_sq + totals
    return (column_block, diagonal_inv)


def solution(mesh):
    in_specs = (P(None, "row", "col"), P(None, "col", None), P(None, "row", None), P())
    out_specs = (P(None, ("row", "col"), None), P())
    return jax.shard_map(
        per_device, mesh=mesh, in_specs=in_specs, out_specs=out_specs, check_vma=False
    )
```

profile of v0, /device:TPU:1, one launch (start us, length us, event | category | flops | bytes accessed | tf_op | source)
XLA Modules:
  0.0 400.9 jit_solution(441896261909000590)
XLA Ops:
  7.2 0.0 copy-start
  7.2 0.0 copy-start.2
  7.2 0.0 all-gather.3.cloned.1.call-start
  7.2 0.7 all-gather.3.cloned.1.call-update
  7.9 0.0 all-gather.5.cloned.1.call-start
  8.0 65.1 %all-gather.3.cloned.1.call-done = f32[2,512,512]{2,1,0:T(8,128)} async-done(((f32[2,64,512]{2,1,0:T(8,128)}), f32[2,512,512]{2,1,0:T(8,128)}) %all-gather.3.cloned.1.call-update) | async-done | bytes 2097168 | tf_op jit(solution)/shard_map/all_gather | solution.py:41
  73.1 3.9 fusion.16
  76.9 0.0 all-gather.5.cloned.1.call-update
  77.0 0.0 reduce-scatter.2.cloned.1.call-start
  77.0 0.0 copy-done.2
  77.0 0.1 copy.15
  77.1 14.1 %gather_fusion = s32[4096,2]{1,0:T(8,128)} fusion(s32[2,16]{0,1:T(8,128)S(1)} %copy.15, s32[4096]{0:T(1024)S(1)} %broadcast_clamp_fusion), kind=kCustom, calls=%fused_computation | custom fusion | bytes 81920 | tf_op jit(solution)/shard_map/jit(_take)/gather | solution.py:29
  91.2 6.2 %compare_select_fusion.1 = (s32[2,4096,1]{0,1,2:T(8,128)}, s32[2,4096,1]{0,1,2:T(8,128)S(1)}) fusion(s32[4096,2]{1,0:T(8,128)} %gather_fusion, s32[]{:T(128)S(6)} %mul.31, s32[4096]{0:T(1024)S(1)} %fusion.6, pred[4096]{0:T(1024)(128)(4,1)S(1)} %fusion.15, s32[]{:T(128)S(6)} %mul.33), kind=kLoop, calls=%fused_computation.4 | loop fusion | flops 155648 | bytes 118792 | tf_op jit(solution)/shard_map/vmap()/select_n | solution.py:14
  97.4 0.0 copy-start.5
  97.4 0.0 copy-start.6
  97.4 2.3 copy.16
  99.7 0.0 copy-start.3
  99.7 0.0 copy-start.4
  99.7 0.6 copy.20
  100.4 0.0 copy-done.5
  100.4 0.0 copy-done.6
  100.4 0.3 and_reduce_fusion
  100.7 1.5 copy.26
  102.2 0.8 copy.24
  103.1 0.0 copy-done.3
  103.1 0.0 copy-done.4
  103.1 0.3 multiply_reduce_fusion.2
  103.4 0.6 copy.27
  104.0 2.6 broadcast_select_fusion
  106.6 2.2 copy.23
  108.8 0.7 copy.25
  109.5 1.5 broadcast_select_fusion.1
  111.0 2.2 copy.19
  113.2 62.4 %all-gather.5.cloned.1.call-done = f32[2,4096,512]{2,1,0:T(8,128)} async-done(((f32[2,128,512]{2,1,0:T(8,128)}), f32[2,4096,512]{2,1,0:T(8,128)}) %all-gather.5.cloned.1.call-update) | async-done | bytes 16777232 | tf_op jit(solution)/shard_map/all_gather | solution.py:26
  175.6 49.8 %scatter_custom_fusion.1 = f32[1024,512]{1,0:T(8,128)S(1)} fusion(s32[8192]{0:T(1024)S(1)} %bitcast.31, f32[8192,512]{1,0:T(8,128)} %bitcast.33, f32[]{:T(128)} %constant.54.clone.1), kind=kCustom, calls=%fused_computation.11 | custom fusion | flops 4194304 | bytes 2097664
  225.4 49.2 %scatter_custom_fusion = f32[256,512]{1,0:T(8,128)S(1)} fusion(s32[8192]{0:T(1024)S(1)} %bitcast.32, f32[8192,512]{1,0:T(8,128)} %bitcast.34, f32[]{:T(128)} %constant.54.clone.1), kind=kCustom, calls=%fused_computation.15 | custom fusion | flops 4194304 | bytes 524800
  274.7 0.0 copy-done
  274.7 3.2 multiply_reduce_fusion
  277.9 0.0 copy-start.1
  277.9 0.0 reduce-scatter.2.cloned.1.call-update
  277.9 1.6 copy-done.1
  279.5 0.2 multiply_reduce_fusion.1
  279.7 78.5 %psum.7 = f32[2,512]{1,0:T(2,128)S(1)} all-reduce(f32[2,512]{1,0:T(2,128)S(1)} %get-tuple-element.8), channel_id=1, replica_groups=mesh['row'=8,'col'=32] {'row','col'}, use_global_device_ids=true, to_apply=%region_5.6 | all-reduce | flops 1024 | bytes 8192 | tf_op jit(solution)/shard_map/psum | solution.py:48
  358.2 0.6 add.100
  358.8 34.1 %reduce-scatter.2.cloned.1.call-done = f32[2,16,512]{2,1,0:T(8,128)} async-done(((f32[2,512,512]{2,1,0:T(8,128)}), f32[2,16,512]{2,1,0:T(8,128)}) %reduce-scatter.2.cloned.1.call-update) | async-done | bytes 65552 | tf_op jit(solution)/shard_map/reduce_scatter | solution.py:45
  392.9 1.5 neg.3
  (7 shorter events, 0.1 us)
Async XLA Ops:
  7.2 267.5 %copy-start = (f32[2,512,128]{2,1,0:T(8,128)S(1)}, f32[2,512,128]{2,1,0:T(8,128)}, u32[]{:S(2)}) copy-start(f32[2,512,128]{2,1,0:T(8,128)} %param.4) | copy-start | bytes 1572868
  7.2 69.8 %copy-start.2 = (s32[2,16]{1,0:T(2,128)S(1)}, s32[2,16]{1,0:T(2,128)}, u32[]{:S(2)}) copy-start(s32[2,16]{1,0:T(2,128)} %param.7) | copy-start | bytes 388
  7.2 65.9 %all-gather.3.cloned.1.call-start = ((), (), s32[]{:S(2)}) async-start(), calls=%async_computation.1 | async-start | bytes 2359296 | tf_op jit(solution)/shard_map/all_gather | solution.py:41
  7.9 167.7 %all-gather.5.cloned.1.call-start = ((), (), s32[]{:S(2)}) async-start(), calls=%async_computation.2 | async-start | bytes 17301504 | tf_op jit(solution)/shard_map/all_gather | solution.py:26
  77.0 316.0 %reduce-scatter.2.cloned.1.call-start = ((), (), s32[]{:S(2)}) async-start(), calls=%async_computation.3 | async-start | bytes 2162688 | tf_op jit(solution)/shard_map/reduce_scatter | solution.py:45
  97.4 3.0 copy-start.5
  97.4 3.0 copy-start.6
  99.7 3.4 copy-start.3
  99.7 3.4 copy-start.4
  277.9 1.6 copy-start.1
Sparse Core Ops, SparseCore 0:
  10.6 62.4 all-gather.2
  77.1 98.4 all-gather.4
  278.0 114.8 reduce-scatter.1
where the time goes:
time: 405 us; the launch traced here: 401 us
  waiting for transfers between devices  162 us (40%)
  other arithmetic  112 us (28%)
  blocking collectives  78.5 us (19%)
  local copies, waits for them, and re-layouts  26.8 us (7%)
  between operations  13.9 us (3%)
  matrix products  7.07 us (2%)
    unnamed x6, other arithmetic  104 us
    psum x1, blocking collectives, per_device(): totals = lax.psum(local_terms, ('row', 'col'))  78.5 us
    all_gather x1, waiting for transfers between devices, per_device(): full_inverse = lax.all_gather(factor_inv, 'row', axis=1, tiled=True)  65.1 us
    all_gather x1, waiting for transfers between devices, spread_tiles(): pieces = lax.all_gather(moving, 'col', axis=1, tiled=True)  62.4 us
    reduce_scatter x1, waiting for transfers between devices, per_device(): lax.psum_scatter(partial_value, 'col', scatter_dimension=1, tiled=True)  34.1 us
    gather x1, local copies, waits for them, and re-layouts, spread_tiles(): jnp.take(pattern, global_rows // B, axis=1) * B + global_rows % B  14.1 us
    unnamed x24, local copies, waits for them, and re-layouts  9.82 us
  transfers between devices with their start and end apart: 3, of which 3 were waited for; matrix products, arithmetic and copies ran while one was open for 9% of the time, Pallas kernels for 0%

commit v1 on v0

v1 whole, which is shorter than its diff:
```python
import jax
import jax.numpy as jnp
from jax import lax
from jax.experimental import pallas as pl
from jax.experimental.pallas import tpu as pltpu
from jax.sharding import PartitionSpec as P


MESH = pl.DeviceIdType.MESH
F32 = jnp.float32
BF16 = jnp.bfloat16

(
    A_RECV, A_SEND, B_RECV, B_SEND, C_RECV_UP, C_RECV_DOWN, C_RECV_UP2, C_RECV_DOWN2,
    C_SEND_UP, C_SEND_DOWN, C_SEND_UP2, C_SEND_DOWN2, ANC_RECV, ANC_SEND_CORE, ANC_SEND_X0, ANC_SEND_X1,
    F_OWN, F_RECV_UP, F_RECV_DOWN, F_RECV_UP2, F_RECV_DOWN2, F_SEND_UP, F_SEND_DOWN, F_SEND_UP2, F_SEND_DOWN2,
    FX_RECV, FX_SEND, PD_RECV, PD_SEND0, PD_SEND1, Y_RECV, Y_SEND, O_RECV, O_SEND, D1_RECV, D1_SEND, D2_RECV, D2_SEND,
    N_SEMS,
) = range(39)


def halves(x):
    high = x.astype(BF16)
    low = (x - high.astype(F32)).astype(BF16)
    return high, low


def dot3(a_high, a_low, b_high, b_low):
    def dot(a, b):
        return jnp.dot(a, b, preferred_element_type=F32)

    return dot(a_high, b_high) + (dot(a_low, b_high) + dot(a_high, b_low))


def kernel(
    anc, pan, fin, pat, out_block, out_diag,
    inv, buf_a, send_b, pbuf, abuf, fbuf, cbuf, rs_up, rs_down, ysum, ybuf, pdiag, spread, prod, d_send, d1, d1_sum, d2,
    a_high, a_low, f_high, f_low, sem, rs_recv, rs_send,
):
    r = lax.axis_index("row")
    c = lax.axis_index("col")
    y, xh = r // 2, r % 2
    z, xl, k = c // 4, (c // 2) % 2, c % 2
    q = 2 * z + xl
    y_up, y_down = (y + 1) % 4, (y + 3) % 4
    z_up, z_down = (z + 1) % 8, (z + 7) % 8

    def col(z_, xl_, k_):
        return z_ * 4 + xl_ * 2 + k_

    def remote(src, dst, send_sem, recv_sem, row_, col_):
        return pltpu.make_async_remote_copy(
            src_ref=src, dst_ref=dst, send_sem=send_sem, recv_sem=recv_sem, device_id=(row_, col_), device_id_type=MESH
        )

    def wait_bytes(ref, s):
        pltpu.make_async_copy(ref, ref, s).wait()

    def start_either(src, dst, send_sem, recv_sem, row_, col_):
        mine = jnp.logical_and(row_ == r, col_ == c)

        @pl.when(mine)
        def _():
            pltpu.make_async_copy(src, dst, recv_sem).start()

        @pl.when(jnp.logical_not(mine))
        def _():
            remote(src, dst, send_sem, recv_sem, row_, col_).start()

    pd_src_row = 2 * ((z % 2) * 2 + xl) + (z % 4) // 2

    with jax.named_scope("greet"):
        barrier = pltpu.get_barrier_semaphore()

        def greet(row_, col_):
            pl.semaphore_signal(barrier, inc=1, device_id=(row_, col_), device_id_type=MESH)

        def greet_col(j, carry):
            greet(r, (c + j) % 32)
            return carry

        lax.fori_loop(1, 32, greet_col, 0)

        def greet_row(j, carry):
            greet((r + j) % 8, c)
            greet((r + j) % 8, col(z, xl, 1 - k))
            return carry

        lax.fori_loop(1, 8, greet_row, 0)
        greet(2 * y + 1 - xh, col(z, 1 - xl, k))
        for x_src in range(2):
            src_col = col(r, x_src, k)

            @pl.when(jnp.logical_not(jnp.logical_and(pd_src_row == r, src_col == c)))
            def _():
                greet(pd_src_row, src_col)

        others = 31 + 14 + 1
        for t in range(2):
            dst_col = col(4 * t + 2 * xh + y // 2, y % 2, k)
            mine = jnp.logical_and(z == r, dst_col == c)
            others = others + jnp.where(mine, jnp.int32(0), jnp.int32(1))
        pl.semaphore_wait(barrier, others)

    with jax.named_scope("start"):
        def send_a(j, carry):
            zi, xi, s = 4 * k + j // 4, (j // 2) % 2, j % 2
            src = pan.at[
                s, pl.ds(pl.multiple_of(32 * y + 8 * (j // 4), 8), 8), pl.ds(pl.multiple_of(256 * xi, 256), 256)
            ]
            start_either(src, buf_a.at[q], sem.at[A_SEND], sem.at[A_RECV], r, col(zi, xi, s))
            return carry

        lax.fori_loop(0, 16, send_a, 0)

        f_own = pltpu.make_async_copy(fin.at[k], fbuf.at[y, xh], sem.at[F_OWN])
        f_own.start()
        f_up = remote(fin.at[k], fbuf.at[y, xh], sem.at[F_SEND_UP], sem.at[F_RECV_UP], 2 * y_up + xh, c)
        f_down = remote(fin.at[k], fbuf.at[y, xh], sem.at[F_SEND_DOWN], sem.at[F_RECV_DOWN], 2 * y_down + xh, c)
        f_up.start()
        f_down.start()

        quarter = abuf.at[2 * xl + k]
        pltpu.make_async_copy(anc.at[k], quarter, sem.at[ANC_RECV]).start()
        anc_core = remote(anc.at[1 - k], quarter, sem.at[ANC_SEND_CORE], sem.at[ANC_RECV], r, col(z, xl, 1 - k))
        anc_x0 = remote(anc.at[0], quarter, sem.at[ANC_SEND_X0], sem.at[ANC_RECV], r, col(z, 1 - xl, 0))
        anc_x1 = remote(anc.at[1], quarter, sem.at[ANC_SEND_X1], sem.at[ANC_RECV], r, col(z, 1 - xl, 1))
        anc_core.start()
        anc_x0.start()
        anc_x1.start()

        def invert(n, carry):
            total = jnp.int32(0)
            for j in range(16):
                total = jnp.where(pat[k, j] == n, jnp.int32(j), total)
            inv[n] = total
            return carry

        lax.fori_loop(0, 16, invert, 0)

    with jax.named_scope("wait_a"):
        wait_bytes(buf_a, sem.at[A_RECV])

    with jax.named_scope("send_b"):
        b_dst = pbuf.at[:, z // 4, y, pl.ds(pl.multiple_of(8 * (z % 4), 8), 8), :]

        def send_b_to(j, carry):
            zd = (z + j) % 8
            send_b[zd, 0] = buf_a[inv[2 * zd]]
            send_b[zd, 1] = buf_a[inv[2 * zd + 1]]
            remote(send_b.at[zd], b_dst, sem.at[B_SEND], sem.at[B_RECV], r, col(zd, xl, k)).start()
            return carry

        lax.fori_loop(1, 8, send_b_to, 0)
        send_b[z, 0] = buf_a[inv[2 * z]]
        send_b[z, 1] = buf_a[inv[2 * z + 1]]
        pltpu.make_async_copy(send_b.at[z], b_dst, sem.at[B_RECV]).start()

    with jax.named_scope("wait_b"):
        wait_bytes(pbuf.at[:, :, y], sem.at[B_RECV])

    with jax.named_scope("send_c"):
        c_up = remote(
            pbuf.at[:, :, y], pbuf.at[:, :, y], sem.at[C_SEND_UP], sem.at[C_RECV_UP], 2 * y_up + xh, c
        )
        c_down = remote(
            pbuf.at[:, :, y], pbuf.at[:, :, y], sem.at[C_SEND_DOWN], sem.at[C_RECV_DOWN], 2 * y_down + xh, c
        )
        c_up.start()
        c_down.start()
        for t in range(2):
            start_either(
                pbuf.at[t, xh, y], pdiag.at[xl], sem.at[PD_SEND0 + t], sem.at[PD_RECV],
                z, col(4 * t + 2 * xh + y // 2, y % 2, k),
            )

    with jax.named_scope("factor_y"):
        wait_bytes(fbuf.at[y_down, xh], sem.at[F_RECV_UP])
        f_up2 = remote(
            fbuf.at[y_down, xh, pl.ds(0, 32)], fbuf.at[y_down, xh, pl.ds(0, 32)],
            sem.at[F_SEND_UP2], sem.at[F_RECV_UP2], 2 * y_up + xh, c,
        )
        f_up2.start()
        wait_bytes(fbuf.at[y_up, xh], sem.at[F_RECV_DOWN])
        f_down2 = remote(
            fbuf.at[y_up, xh, pl.ds(32, 32)], fbuf.at[y_up, xh, pl.ds(32, 32)],
            sem.at[F_SEND_DOWN2], sem.at[F_RECV_DOWN2], 2 * y_down + xh, c,
        )
        f_down2.start()

    with jax.named_scope("wait_c"):
        wait_bytes(pbuf.at[:, :, y_down], sem.at[C_RECV_UP])
        c_up2 = remote(
            pbuf.at[0, :, y_down], pbuf.at[0, :, y_down], sem.at[C_SEND_UP2], sem.at[C_RECV_UP2], 2 * y_up + xh, c
        )
        c_up2.start()
        wait_bytes(pbuf.at[:, :, y_up], sem.at[C_RECV_DOWN])
        c_down2 = remote(
            pbuf.at[1, :, y_up], pbuf.at[1, :, y_up], sem.at[C_SEND_DOWN2], sem.at[C_RECV_DOWN2], 2 * y_down + xh, c
        )
        c_down2.start()

    with jax.named_scope("factor_x"):
        f_own.wait()
        y_far = (y + 2) % 4
        wait_bytes(fbuf.at[y_far, xh, pl.ds(0, 32)], sem.at[F_RECV_UP2])
        wait_bytes(fbuf.at[y_far, xh, pl.ds(32, 32)], sem.at[F_RECV_DOWN2])
        f_x = remote(
            fbuf.at[:, xh], fbuf.at[:, xh], sem.at[FX_SEND], sem.at[FX_RECV], 2 * y + 1 - xh, col(z, 1 - xl, k)
        )
        f_x.start()

    with jax.named_scope("wait_anc"):
        wait_bytes(abuf, sem.at[ANC_RECV])
        for j in range(4):
            high, low = halves(abuf[j])
            a_high[:, 128 * j : 128 * j + 128] = high
            a_low[:, 128 * j : 128 * j + 128] = low

    with jax.named_scope("wait_c2"):
        wait_bytes(pbuf.at[0, :, y_far], sem.at[C_RECV_UP2])
        wait_bytes(pbuf.at[1, :, y_far], sem.at[C_RECV_DOWN2])

    with jax.named_scope("product"):
        p_high, p_low = halves(pbuf[...].reshape(512, 256))
        cbuf[...] = dot3(a_high[...], a_low[...], p_high, p_low).reshape(8, 64, 256)

    sends = []

    def rs_step(step):
        distance = 4 - step
        for sub in range(2):
            rows = pl.ds(32 * sub, 32)
            for way in range(2):
                buf = (rs_up, rs_down)[way]
                zd = (z + distance) % 8 if way == 0 else (z + 8 - distance) % 8
                to = z_up if way == 0 else z_down
                half = pl.ds(128 * way, 128)
                if step == 0:
                    cols = half
                else:
                    cols = pl.ds(0, 256)
                    before = half if step == 1 else pl.ds(0, 256)
                    wait_bytes(buf.at[step - 1, rows, before], rs_recv.at[way, step - 1, sub])
                    cbuf[zd, rows, before] += buf[step - 1, rows, before]
                copy = remote(
                    cbuf.at[zd, rows, cols], buf.at[step, rows, cols],
                    rs_send.at[way, step, sub], rs_recv.at[way, step, sub], r, col(to, xl, k),
                )
                copy.start()
                sends.append(copy)

    with jax.named_scope("reduce0"):
        rs_step(0)
    with jax.named_scope("reduce1"):
        rs_step(1)
    with jax.named_scope("factor"):
        wait_bytes(fbuf.at[:, 1 - xh], sem.at[FX_RECV])
        factor = fbuf[...].reshape(512, 512)
        high, low = halves(factor)
        f_high[...] = high
        f_low[...] = low
    with jax.named_scope("reduce2"):
        rs_step(2)
    with jax.named_scope("spread"):
        wait_bytes(pdiag, sem.at[PD_RECV])
        s_high, s_low = halves(jnp.concatenate([pdiag[0], pdiag[1]], axis=1))
        spread[...] = dot3(s_high, s_low, f_high[...], f_low[...])
    with jax.named_scope("reduce3"):
        rs_step(3)
    with jax.named_scope("reduce4"):
        for sub in range(2):
            rows = pl.ds(32 * sub, 32)
            for way in range(2):
                wait_bytes((rs_up, rs_down)[way].at[3, rows, :], rs_recv.at[way, 3, sub])
            ysum[sub] = cbuf[z, rows, :] + (rs_up[3, rows, :] + rs_down[3, rows, :])
        y_copy = remote(ysum.at[1 - xl], ybuf.at[xl], sem.at[Y_SEND], sem.at[Y_RECV], r, col(z, 1 - xl, k))
        y_copy.start()
        ybuf[xl] = ysum[xl]
        wait_bytes(ybuf.at[1 - xl], sem.at[Y_RECV])

    with jax.named_scope("apply_factor"):
        y_high, y_low = halves(jnp.concatenate([ybuf[0], ybuf[1]], axis=1))
        result = dot3(y_high, y_low, f_high[...], f_low[...])
        prod[...] = -result.reshape(2, 16, 512)
        o_copy = remote(prod.at[1 - k], out_block.at[k], sem.at[O_SEND], sem.at[O_RECV], r, col(z, xl, 1 - k))
        o_copy.start()
        d_send[...] = jnp.sum(spread[...] * result, axis=0, keepdims=True)
        d1[q] = d_send[...]

    with jax.named_scope("diag_col"):
        def send_d1(j, carry):
            remote(d_send, d1.at[q], sem.at[D1_SEND], sem.at[D1_RECV], r, (c + 2 * j) % 32).start()
            return carry

        lax.fori_loop(1, 16, send_d1, 0)
        out_block[k] = prod[k]
        own_factor = fbuf[y, xh]
        own_sq = jnp.sum(own_factor * own_factor, axis=0, keepdims=True)
        wait_bytes(d1.at[pl.ds(0, 15)], sem.at[D1_RECV])
        d1_sum[...] = jnp.sum(d1[...], axis=0) + own_sq
        d2[k, r] = d1_sum[...]

    with jax.named_scope("diag_row"):
        def send_d2(j, carry):
            remote(d1_sum, d2.at[k, r], sem.at[D2_SEND], sem.at[D2_RECV], (r + j) % 8, c).start()
            remote(d1_sum, d2.at[k, r], sem.at[D2_SEND], sem.at[D2_RECV], (r + j) % 8, col(z, xl, 1 - k)).start()
            return carry

        lax.fori_loop(1, 8, send_d2, 0)
        remote(d1_sum, d2.at[k, r], sem.at[D2_SEND], sem.at[D2_RECV], r, col(z, xl, 1 - k)).start()
        wait_bytes(d1.at[pl.ds(0, 15)], sem.at[D2_RECV])
        for s in range(2):
            out_diag[pl.ds(s, 1), :] = jnp.sum(d2[s], axis=0)

    with jax.named_scope("finish"):
        wait_bytes(out_block.at[1 - k], sem.at[O_RECV])
        for copy in [f_up, f_down, f_up2, f_down2, f_x, anc_core, anc_x0, anc_x1, c_up, c_down, c_up2, c_down2, y_copy, o_copy] + sends:
            copy.wait_send()
        wait_bytes(d1.at[pl.ds(0, 15)], sem.at[D1_SEND])
        wait_bytes(d1.at[pl.ds(0, 15)], sem.at[D2_SEND])
        wait_bytes(send_b.at[pl.ds(0, 7)], sem.at[B_SEND])
        a_self = z // 4 == k

        @pl.when(a_self)
        def _():
            wait_bytes(buf_a.at[pl.ds(0, 15)], sem.at[A_SEND])

        @pl.when(jnp.logical_not(a_self))
        def _():
            wait_bytes(buf_a, sem.at[A_SEND])

        for t in range(2):
            dst_col = col(4 * t + 2 * xh + y // 2, y % 2, k)

            @pl.when(jnp.logical_not(jnp.logical_and(z == r, dst_col == c)))
            def _():
                wait_bytes(pdiag.at[0], sem.at[PD_SEND0 + t])


def per_device(ancestor, panel, factor_inv, pattern):
    vmem = pltpu.VMEM
    return pl.pallas_call(
        kernel,
        out_shape=(jax.ShapeDtypeStruct((2, 16, 512), F32), jax.ShapeDtypeStruct((2, 512), F32)),
        in_specs=[pl.BlockSpec(memory_space=pl.ANY)] * 3 + [pl.BlockSpec(memory_space=pltpu.SMEM)],
        out_specs=(pl.BlockSpec(memory_space=vmem), pl.BlockSpec(memory_space=vmem)),
        scratch_shapes=[
            pltpu.SMEM((16,), jnp.int32),
            vmem((16, 8, 256), F32),
            vmem((8, 2, 8, 256), F32),
            vmem((2, 2, 4, 32, 256), F32),
            vmem((4, 512, 128), F32),
            vmem((4, 2, 64, 512), F32),
            vmem((8, 64, 256), F32),
            vmem((4, 64, 256), F32),
            vmem((4, 64, 256), F32),
            vmem((2, 32, 256), F32),
            vmem((2, 32, 256), F32),
            vmem((2, 32, 256), F32),
            vmem((32, 512), F32),
            vmem((2, 16, 512), F32),
            vmem((1, 512), F32),
            vmem((16, 1, 512), F32),
            vmem((1, 512), F32),
            vmem((2, 8, 1, 512), F32),
            vmem((512, 512), BF16),
            vmem((512, 512), BF16),
            vmem((512, 512), BF16),
            vmem((512, 512), BF16),
            pltpu.SemaphoreType.DMA((N_SEMS,)),
            pltpu.SemaphoreType.DMA((2, 4, 2)),
            pltpu.SemaphoreType.DMA((2, 4, 2)),
        ],
        compiler_params=pltpu.CompilerParams(
            collective_id=0, has_side_effects=True, vmem_limit_bytes=32 * 1024 * 1024
        ),
    )(ancestor, panel, factor_inv, pattern)


def solution(mesh):
    in_specs = (P(None, "row", "col"), P(None, "col", None), P(None, "row", None), P())
    out_specs = (P(None, ("row", "col"), None), P())
    return jax.shard_map(per_device, mesh=mesh, in_specs=in_specs, out_specs=out_specs, check_vma=False)
```

time: 405 us -> 72.7 us (0.18)
  waiting for transfers between devices: 162 us -> 0 us
  other arithmetic: 112 us -> 0 us
  blocking collectives: 78.5 us -> 0 us
  Pallas kernels: 0 us -> 66.9 us
  local copies, waits for them, and re-layouts: 26.8 us -> 4.93 us
  between operations: 13.9 us -> 0.65 us
  matrix products: 7.07 us -> 0 us
    all_gather x2 -> x0, waiting for transfers between devices: 128 us -> none  [the longest x1 65.1 us: per_device(): full_inverse = lax.all_gather(factor_inv, 'row', axis=1, tiled=True)]
    unnamed x6 -> x0, other arithmetic: 104 us -> none
    psum x1 -> x0, blocking collectives: 78.5 us -> none  [per_device(): totals = lax.psum(local_terms, ('row', 'col'))]
    pallas_call x0 -> x1, Pallas kernels: none -> 66.9 us  [per_device(): pl.pallas_call(kernel, out_shape=(jax.ShapeDtypeStruct((2, 16, 512), F32)...]
    reduce_scatter x1 -> x0, waiting for transfers between devices: 34.1 us -> none  [per_device(): lax.psum_scatter(partial_value, 'col', scatter_dimension=1, tiled=True)]
    gather x1 -> x0, local copies, waits for them, and re-layouts: 14.1 us -> none  [spread_tiles(): jnp.take(pattern, global_rows // B, axis=1) * B + global_rows % B]
    dot_general x2 -> x0, matrix products: 7.07 us -> none  [the longest x1 3.85 us: per_device(): moving = jnp.einsum('srw,swv->srv', panel, full_inverse, precision=highest)]
    select_n x3 -> x0, other arithmetic: 6.22 us -> none  [the longest x1 6.19 us: one_group(): return accum.at[target].add(values, mode='drop')]
  transfers between devices with their start and end apart: 3 -> 0, of which waited for: 3 -> 0; matrix products, arithmetic and copies ran while one was open for 9% -> 0% of each run, Pallas kernels for 0% -> 0%
where the time goes in v1:
time: 72.7 us; the launch traced here: 72.5 us
  Pallas kernels  66.9 us (92%)
  local copies, waits for them, and re-layouts  4.93 us (7%)
    pallas_call x1, Pallas kernels, per_device(): pl.pallas_call(kernel, out_shape=(jax.ShapeDtypeStruct((2, 16, 512), F32)...  66.9 us
    unnamed x10, local copies, waits for them, and re-layouts  4.93 us

profile of v1, /device:TPU:1, one launch (start us, length us, event | category | flops | bytes accessed | tf_op | source)
XLA Modules:
  0.0 72.5 jit_solution(16572197908527898505)
XLA Ops:
  0.6 0.0 copy-start
  0.6 1.0 %copy-done = f32[2,512,128]{2,1,0:T(8,128)S(1)} copy-done((f32[2,512,128]{2,1,0:T(8,128)S(1)}, f32[2,512,128]{2,1,0:T(8,128)}, u32[]{:S(2)}) %copy-start) | copy-done | bytes 524312
  1.7 0.0 copy-start.1
  1.7 1.0 %copy-done.1 = f32[2,128,512]{2,1,0:T(8,128)S(1)} copy-done((f32[2,128,512]{2,1,0:T(8,128)S(1)}, f32[2,128,512]{2,1,0:T(8,128)}, u32[]{:S(2)}) %copy-start.1) | copy-done | bytes 524312
  2.7 0.0 copy-start.2
  2.7 0.9 %copy-done.2 = f32[2,64,512]{2,1,0:T(8,128)S(1)} copy-done((f32[2,64,512]{2,1,0:T(8,128)S(1)}, f32[2,64,512]{2,1,0:T(8,128)}, u32[]{:S(2)}) %copy-start.2) | copy-done | bytes 262168
  3.7 0.0 copy-start.3
  3.7 0.7 copy-done.3
  4.3 66.9 %shard_map.59 = (f32[2,16,512]{2,1,0:T(8,128)S(1)}, f32[2,512]{1,0:T(2,128)S(1)}) custom-call(f32[2,512,128]{2,1,0:T(8,128)S(1)} %copy-done, f32[2,128,512]{2,1,0:T(8,128)S(1)} %copy-done.1, f32[2,64,512]{2,1,0:T(8,128)S(1)} %copy-done.2, s32[2,16]{1,0:T(2,128)S(1)} %copy-done.3), custom_call_target="tpu_custom_call" | custom-call | tf_op jit(solution)/shard_map/pallas_call | solution.py:343
  71.3 0.6 copy.8
  71.9 0.6 copy.9
Async XLA Ops:
  0.6 1.0 %copy-start = (f32[2,512,128]{2,1,0:T(8,128)S(1)}, f32[2,512,128]{2,1,0:T(8,128)}, u32[]{:S(2)}) copy-start(f32[2,512,128]{2,1,0:T(8,128)} %anc.1) | copy-start | bytes 1572868
  1.7 1.0 %copy-start.1 = (f32[2,128,512]{2,1,0:T(8,128)S(1)}, f32[2,128,512]{2,1,0:T(8,128)}, u32[]{:S(2)}) copy-start(f32[2,128,512]{2,1,0:T(8,128)} %pan.1) | copy-start | bytes 1572868
  2.7 0.9 %copy-start.2 = (f32[2,64,512]{2,1,0:T(8,128)S(1)}, f32[2,64,512]{2,1,0:T(8,128)}, u32[]{:S(2)}) copy-start(f32[2,64,512]{2,1,0:T(8,128)} %fin.1) | copy-start | bytes 786436
  3.7 0.7 copy-start.3

commit v2 on v0

v2 whole, which is shorter than its diff:
```python
import jax
import jax.numpy as jnp
from jax import lax
from jax.experimental import pallas as pl
from jax.experimental.pallas import tpu as pltpu
from jax.sharding import PartitionSpec as P


MESH = pl.DeviceIdType.MESH
F32 = jnp.float32
BF16 = jnp.bfloat16
STOP = ""


def halves(x):
    high = x.astype(BF16)
    low = (x - high.astype(F32)).astype(BF16)
    return high, low


def dot3(a_high, a_low, b_high, b_low):
    def dot(a, b):
        return jnp.dot(a, b, preferred_element_type=F32)

    return dot(a_high, b_high) + (dot(a_low, b_high) + dot(a_high, b_low))


def kernel(
    anc, pan, fin, pat_hbm, out_block, out_diag,
    pat, inv, buf_a, send_b, pbuf, abuf, fbuf, cbuf, rbuf, pdiag, spread, prod, d_send, own_sq, d1, d1_sum, d2,
    a_high, a_low, f_high, f_low, sems,
):
    r = lax.axis_index("row")
    c = lax.axis_index("col")
    y, xh = r // 2, r % 2
    z, xl, k = c // 4, (c // 2) % 2, c % 2
    q = 2 * z + xl

    names = {}
    pending = {}

    def sem(name):
        return sems.at[names.setdefault(name, len(names))]

    def col(z_, xl_, k_):
        return z_ * 4 + xl_ * 2 + k_

    def remote(src, dst, send_sem, recv_sem, row_, col_):
        return pltpu.make_async_remote_copy(
            src_ref=src, dst_ref=dst, send_sem=send_sem, recv_sem=recv_sem, device_id=(row_, col_), device_id_type=MESH
        )

    def expect(name, ref):
        pending[name] = lambda: pltpu.make_async_copy(ref, ref, sem(name)).wait()

    def need(*keys):
        for key in keys:
            pending.pop(key)()

    def send(name, src, dst, row_, col_, arrives):
        copy = remote(src, dst, sem(name + ".send"), sem(name), row_, col_)
        copy.start()
        pending[name + ".send"] = copy.wait_send
        if arrives is not None:
            expect(name, arrives)

    def start_either(src, dst, send_sem, recv_sem, row_, col_):
        mine = jnp.logical_and(row_ == r, col_ == c)

        @pl.when(mine)
        def _():
            pltpu.make_async_copy(src, dst, recv_sem).start()

        @pl.when(jnp.logical_not(mine))
        def _():
            remote(src, dst, send_sem, recv_sem, row_, col_).start()

    def body():
        pat_copy = pltpu.make_async_copy(pat_hbm, pat, sem("pat"))
        pat_copy.start()
        pending["pat"] = pat_copy.wait

        barrier = pltpu.get_barrier_semaphore()

        def greet(row_, col_):
            pl.semaphore_signal(barrier, inc=1, device_id=(row_, col_), device_id_type=MESH)

        def greet_col(j, carry):
            greet(r, (c + j) % 32)
            return carry

        lax.fori_loop(1, 32, greet_col, 0)

        def greet_row(j, carry):
            greet((r + j) % 8, c)
            greet((r + j) % 8, col(z, xl, 1 - k))
            return carry

        lax.fori_loop(1, 8, greet_row, 0)
        greet(2 * y + 1 - xh, col(z, 1 - xl, k))
        pd_src_row = 2 * ((z % 2) * 2 + xl) + (z % 4) // 2
        for x_src in range(2):
            src_col = col(r, x_src, k)

            @pl.when(jnp.logical_not(jnp.logical_and(pd_src_row == r, src_col == c)))
            def _():
                greet(pd_src_row, src_col)

        others = 31 + 14 + 1
        pd_mine = []
        for t in range(2):
            mine = jnp.logical_and(z == r, col(4 * t + 2 * xh + y // 2, y % 2, k) == c)
            pd_mine.append(mine)
            others = others + jnp.where(mine, jnp.int32(0), jnp.int32(1))
        pl.semaphore_wait(barrier, others)
        if STOP == "greet":
            return

        def send_a(j, carry):
            zi, xi, s = 4 * k + j // 4, (j // 2) % 2, j % 2
            src = pan.at[
                s, pl.ds(pl.multiple_of(32 * y + 8 * (j // 4), 8), 8), pl.ds(pl.multiple_of(256 * xi, 256), 256)
            ]
            start_either(src, buf_a.at[q], sem("a.send"), sem("a"), r, col(zi, xi, s))
            return carry

        lax.fori_loop(0, 16, send_a, 0)
        expect("a", buf_a)

        def wait_send_a():
            @pl.when(z // 4 == k)
            def _():
                pltpu.make_async_copy(buf_a.at[pl.ds(0, 15)], buf_a.at[pl.ds(0, 15)], sem("a.send")).wait()

            @pl.when(z // 4 != k)
            def _():
                pltpu.make_async_copy(buf_a, buf_a, sem("a.send")).wait()

        pending["a.send"] = wait_send_a
        if STOP == "a_only":
            return

        own = fbuf.at[y, xh]
        f_own = pltpu.make_async_copy(fin.at[k], own, sem("f_own"))
        f_own.start()
        pending["f_own"] = f_own.wait
        for d in (2, 1, 3):
            send("f%d" % d, fin.at[k], own, 2 * ((y + d) % 4) + xh, c, fbuf.at[(y + 4 - d) % 4, xh])

        quarter = abuf.at[2 * xl + k]
        pltpu.make_async_copy(anc.at[k], quarter, sem("anc")).start()
        for name, s, x_to in (("anc_core", 1 - k, xl), ("anc_x0", 0, 1 - xl), ("anc_x1", 1, 1 - xl)):
            copy = remote(anc.at[s], quarter, sem(name), sem("anc"), r, col(z, x_to, s))
            copy.start()
            pending[name] = copy.wait_send
        expect("anc", abuf)

        need("pat")

        def invert(n, carry):
            found = jnp.int32(0)
            for j in range(16):
                found = jnp.where(pat[k, j] == n, jnp.int32(j), found)
            inv[n] = found
            return carry

        lax.fori_loop(0, 16, invert, 0)
        need("a")
        if STOP == "a":
            return

        b_dst = pbuf.at[:, z // 4, y, pl.ds(pl.multiple_of(8 * (z % 4), 8), 8), :]

        def send_b_to(j, carry):
            zd = (z + j) % 8
            send_b[zd, 0] = buf_a[inv[2 * zd]]
            send_b[zd, 1] = buf_a[inv[2 * zd + 1]]
            remote(send_b.at[zd], b_dst, sem("b.send"), sem("b"), r, col(zd, xl, k)).start()
            return carry

        lax.fori_loop(1, 8, send_b_to, 0)
        send_b[z, 0] = buf_a[inv[2 * z]]
        send_b[z, 1] = buf_a[inv[2 * z + 1]]
        pltpu.make_async_copy(send_b.at[z], b_dst, sem("b")).start()
        expect("b", pbuf.at[:, :, y])
        expect("b.send", send_b.at[pl.ds(0, 7)])
        need("f_own", "f1", "f2", "f3")
        send("f_x", fbuf.at[:, xh], fbuf.at[:, xh], 2 * y + 1 - xh, col(z, 1 - xl, k), fbuf.at[:, 1 - xh])
        if STOP == "f_x1":
            return
        need("b")
        if STOP == "b":
            return

        mine = pbuf.at[:, :, y]
        for d in (2, 1, 3):
            send("c%d" % d, mine, mine, 2 * ((y + d) % 4) + xh, c, pbuf.at[:, :, (y + 4 - d) % 4])
        for t in range(2):
            start_either(
                pbuf.at[t, xh, y], pdiag.at[xl], sem("pd%d.send" % t), sem("pd"),
                z, col(4 * t + 2 * xh + y // 2, y % 2, k),
            )

            def wait_send_pd(t=t):
                @pl.when(jnp.logical_not(pd_mine[t]))
                def _():
                    pltpu.make_async_copy(pdiag.at[0], pdiag.at[0], sem("pd%d.send" % t)).wait()

            pending["pd%d.send" % t] = wait_send_pd
        expect("pd", pdiag)

        need("anc")
        if STOP == "anc":
            return
        for j in range(4):
            high, low = halves(abuf[j])
            a_high[:, 128 * j : 128 * j + 128] = high
            a_low[:, 128 * j : 128 * j + 128] = low

        need("c1", "c2", "c3")
        if STOP == "c2":
            return
        p_high, p_low = halves(pbuf[...].reshape(512, 256))
        cbuf[...] = dot3(a_high[...], a_low[...], p_high, p_low).reshape(16, 32, 256)
        if STOP == "product":
            return

        def send_sum(j, carry):
            zd, xd = (z + (j + 2) // 2) % 8, (xl + j) % 2
            remote(
                cbuf.at[2 * zd + xd], rbuf.at[xl, z], sem("sum.send"), sem("sum"), r, col(zd, xd, k)
            ).start()
            return carry

        lax.fori_loop(0, 14, send_sum, 0)
        remote(cbuf.at[2 * z + 1 - xl], rbuf.at[xl, z], sem("sum.send"), sem("sum"), r, col(z, 1 - xl, k)).start()
        all_but_own = cbuf.at[pl.ds(0, 15)]
        expect("sum", all_but_own)
        expect("sum.send", all_but_own)
        rbuf[xl, z] = cbuf[q]
        need("f_x")
        high, low = halves(fbuf[...].reshape(512, 512))
        f_high[...] = high
        f_low[...] = low
        if STOP == "f_x":
            return
        need("pd")
        s_high, s_low = halves(jnp.concatenate([pdiag[0], pdiag[1]], axis=1))
        spread[...] = dot3(s_high, s_low, f_high[...], f_low[...])
        own_factor = fbuf[y, xh]
        own_sq[...] = jnp.sum(own_factor * own_factor, axis=0, keepdims=True)
        if STOP == "spread":
            return
        need("sum")
        if STOP == "sum":
            return

        y_high, y_low = halves(jnp.concatenate([jnp.sum(rbuf[0], axis=0), jnp.sum(rbuf[1], axis=0)], axis=1))
        result = dot3(y_high, y_low, f_high[...], f_low[...])
        prod[...] = -result.reshape(2, 16, 512)
        send("o", prod.at[1 - k], out_block.at[k], r, col(z, xl, 1 - k), out_block.at[1 - k])
        d_send[...] = jnp.sum(spread[...] * result, axis=0, keepdims=True)
        d1[q] = d_send[...]
        if STOP == "apply":
            return

        def send_d1(j, carry):
            remote(d_send, d1.at[q], sem("d1.send"), sem("d1"), r, (c + 2 * j) % 32).start()
            return carry

        lax.fori_loop(1, 16, send_d1, 0)
        some = d1.at[pl.ds(0, 15)]
        expect("d1", some)
        expect("d1.send", some)
        out_block[k] = prod[k]
        need("d1")
        if STOP == "d1":
            return
        d1_sum[...] = jnp.sum(d1[...], axis=0) + own_sq[...]
        d2[k, r] = d1_sum[...]

        def send_d2(j, carry):
            remote(d1_sum, d2.at[k, r], sem("d2.send"), sem("d2"), (r + j) % 8, c).start()
            remote(d1_sum, d2.at[k, r], sem("d2.send"), sem("d2"), (r + j) % 8, col(z, xl, 1 - k)).start()
            return carry

        lax.fori_loop(1, 8, send_d2, 0)
        remote(d1_sum, d2.at[k, r], sem("d2.send"), sem("d2"), r, col(z, xl, 1 - k)).start()
        expect("d2", some)
        expect("d2.send", some)
        need("d2")
        for s in range(2):
            out_diag[pl.ds(s, 1), :] = jnp.sum(d2[s], axis=0)

    body()
    need(*pending)


def per_device(ancestor, panel, factor_inv, pattern):
    vmem = pltpu.VMEM
    return pl.pallas_call(
        kernel,
        out_shape=(jax.ShapeDtypeStruct((2, 16, 512), F32), jax.ShapeDtypeStruct((2, 512), F32)),
        in_specs=[pl.BlockSpec(memory_space=pl.ANY)] * 4,
        out_specs=(pl.BlockSpec(memory_space=vmem), pl.BlockSpec(memory_space=vmem)),
        scratch_shapes=[
            pltpu.SMEM((2, 16), jnp.int32),
            pltpu.SMEM((16,), jnp.int32),
            vmem((16, 8, 256), F32),
            vmem((8, 2, 8, 256), F32),
            vmem((2, 2, 4, 32, 256), F32),
            vmem((4, 512, 128), F32),
            vmem((4, 2, 64, 512), F32),
            vmem((16, 32, 256), F32),
            vmem((2, 8, 32, 256), F32),
            vmem((2, 32, 256), F32),
            vmem((32, 512), F32),
            vmem((2, 16, 512), F32),
            vmem((1, 512), F32),
            vmem((1, 512), F32),
            vmem((16, 1, 512), F32),
            vmem((1, 512), F32),
            vmem((2, 8, 1, 512), F32),
            vmem((512, 512), BF16),
            vmem((512, 512), BF16),
            vmem((512, 512), BF16),
            vmem((512, 512), BF16),
            pltpu.SemaphoreType.DMA((80,)),
        ],
        compiler_params=pltpu.CompilerParams(
            collective_id=0, has_side_effects=True, vmem_limit_bytes=60 * 1024 * 1024
        ),
    )(ancestor, panel, factor_inv, pattern)


def solution(mesh):
    in_specs = (P(None, "row", "col"), P(None, "col", None), P(None, "row", None), P())
    out_specs = (P(None, ("row", "col"), None), P())
    return jax.shard_map(per_device, mesh=mesh, in_specs=in_specs, out_specs=out_specs, check_vma=False)
```

time: 405 us -> 63.6 us (0.16)
  waiting for transfers between devices: 162 us -> 0 us
  other arithmetic: 112 us -> 0 us
  blocking collectives: 78.5 us -> 0 us
  Pallas kernels: 0 us -> 60.8 us
  local copies, waits for them, and re-layouts: 26.8 us -> 2.07 us
  between operations: 13.9 us -> 0.65 us
  matrix products: 7.07 us -> 0 us
    all_gather x2 -> x0, waiting for transfers between devices: 128 us -> none  [the longest x1 65.1 us: per_device(): full_inverse = lax.all_gather(factor_inv, 'row', axis=1, tiled=True)]
    unnamed x6 -> x0, other arithmetic: 104 us -> none
    psum x1 -> x0, blocking collectives: 78.5 us -> none  [per_device(): totals = lax.psum(local_terms, ('row', 'col'))]
    pallas_call x0 -> x1, Pallas kernels: none -> 60.8 us  [per_device(): pl.pallas_call(kernel, out_shape=(jax.ShapeDtypeStruct((2, 16, 512), F32)...]
    reduce_scatter x1 -> x0, waiting for transfers between devices: 34.1 us -> none  [per_device(): lax.psum_scatter(partial_value, 'col', scatter_dimension=1, tiled=True)]
    gather x1 -> x0, local copies, waits for them, and re-layouts: 14.1 us -> none  [spread_tiles(): jnp.take(pattern, global_rows // B, axis=1) * B + global_rows % B]
    unnamed x24 -> x4, local copies, waits for them, and re-layouts: 9.82 us -> 2.07 us
    dot_general x2 -> x0, matrix products: 7.07 us -> none  [the longest x1 3.85 us: per_device(): moving = jnp.einsum('srw,swv->srv', panel, full_inverse, precision=highest)]
  transfers between devices with their start and end apart: 3 -> 0, of which waited for: 3 -> 0; matrix products, arithmetic and copies ran while one was open for 9% -> 0% of each run, Pallas kernels for 0% -> 0%
where the time goes in v2:
time: 63.6 us; the launch traced here: 63.5 us
  Pallas kernels  60.8 us (96%)
  local copies, waits for them, and re-layouts  2.07 us (3%)
  between operations  0.65 us (1%)
    pallas_call x1, Pallas kernels, per_device(): pl.pallas_call(kernel, out_shape=(jax.ShapeDtypeStruct((2, 16, 512), F32)...  60.8 us
    unnamed x4, local copies, waits for them, and re-layouts  2.07 us

profile of v2, /device:TPU:1, one launch (start us, length us, event | category | flops | bytes accessed | tf_op | source)
XLA Modules:
  0.0 63.5 jit_solution(11570420920266583303)
XLA Ops:
  0.6 60.8 %shard_map.59 = (f32[2,16,512]{2,1,0:T(8,128)}, f32[2,512]{1,0:T(2,128)}) custom-call(f32[2,512,128]{2,1,0:T(8,128)} %anc.1, f32[2,128,512]{2,1,0:T(8,128)} %pan.1, f32[2,64,512]{2,1,0:T(8,128)} %fin.1, s32[2,16]{1,0:T(2,128)} %pat_hbm.1), custom_call_target="tpu_custom_call" | custom-call | tf_op jit(solution)/shard_map/pallas_call | solution.py:301
  61.4 0.0 copy-start
  61.4 1.5 %copy.8 = f32[2,16,512]{2,1,0:T(8,128)} copy(f32[2,16,512]{2,1,0:T(8,128)} %get-tuple-element.4) | data formatting | bytes 131072
  62.9 0.0 copy-done
  62.9 0.6 copy.9
Async XLA Ops:
  61.4 1.5 %copy-start = (f32[2,512]{1,0:T(2,128)S(1)}, f32[2,512]{1,0:T(2,128)}, u32[]{:S(2)}) copy-start(f32[2,512]{1,0:T(2,128)} %get-tuple-element.5) | copy-start | bytes 12292

commit v3 on v2

--- a/solution.py
+++ b/solution.py
@@ -9,7 +9,6 @@
 MESH = pl.DeviceIdType.MESH
 F32 = jnp.float32
 BF16 = jnp.bfloat16
-STOP = ""
 
 
 def halves(x):
@@ -25,10 +24,23 @@
     return dot(a_high, b_high) + (dot(a_low, b_high) + dot(a_high, b_low))
 
 
+def times_factor(x, f_high, f_low):
+    high, low = halves(x)
+    both = jnp.concatenate([high, low], axis=0)
+    n = x.shape[0]
+
+    def part(first, cols):
+        rows = slice(first, 512)
+        twice = jnp.dot(both[:, rows], f_high[rows, cols], preferred_element_type=F32)
+        return twice[:n] + (twice[n:] + jnp.dot(high[:, rows], f_low[rows, cols], preferred_element_type=F32))
+
+    return jnp.concatenate([part(0, slice(0, 256)), part(256, slice(256, 512))], axis=1)
+
+
 def kernel(
     anc, pan, fin, pat_hbm, out_block, out_diag,
     pat, inv, buf_a, send_b, pbuf, abuf, fbuf, cbuf, rbuf, pdiag, spread, prod, d_send, own_sq, d1, d1_sum, d2,
-    a_high, a_low, f_high, f_low, sems,
+    a_high, a_low, f_high, f_low, sems, b_sems,
 ):
     r = lax.axis_index("row")
     c = lax.axis_index("col")
@@ -74,6 +86,14 @@
         @pl.when(jnp.logical_not(mine))
         def _():
             remote(src, dst, send_sem, recv_sem, row_, col_).start()
+
+    def far_first(j):
+        half = (j + 1) // 2
+        return 4 + jnp.where(j % 2 == 1, -half, half)
+
+    def near_first(j):
+        half = j // 2 + 1
+        return jnp.where(j % 2 == 0, half, 8 - half)
 
     def body():
         pat_copy = pltpu.make_async_copy(pat_hbm, pat, sem("pat"))
@@ -113,18 +133,20 @@
             pd_mine.append(mine)
             others = others + jnp.where(mine, jnp.int32(0), jnp.int32(1))
         pl.semaphore_wait(barrier, others)
-        if STOP == "greet":
-            return
+
+        def piece(zi, xi, s):
+            return pan.at[
+                s, pl.ds(pl.multiple_of(32 * y + 8 * (zi % 4), 8), 8), pl.ds(pl.multiple_of(256 * xi, 256), 256)
+            ]
 
         def send_a(j, carry):
-            zi, xi, s = 4 * k + j // 4, (j // 2) % 2, j % 2
-            src = pan.at[
-                s, pl.ds(pl.multiple_of(32 * y + 8 * (j // 4), 8), 8), pl.ds(pl.multiple_of(256 * xi, 256), 256)
-            ]
-            start_either(src, buf_a.at[q], sem("a.send"), sem("a"), r, col(zi, xi, s))
-            return carry
-
-        lax.fori_loop(0, 16, send_a, 0)
+            zi, xi, s = 4 * k + (z + j // 4) % 4, (xl + j // 2) % 2, (k + j) % 2
+            remote(piece(zi, xi, s), buf_a.at[q], sem("a.send"), sem("a"), r, col(zi, xi, s)).start()
+            return carry
+
+        lax.fori_loop(1, 16, send_a, 0)
+        first = 4 * k + z % 4
+        start_either(piece(first, xl, k), buf_a.at[q], sem("a.send"), sem("a"), r, col(first, xl, k))
         expect("a", buf_a)
 
         def wait_send_a():
@@ -137,8 +159,6 @@
                 pltpu.make_async_copy(buf_a, buf_a, sem("a.send")).wait()
 
         pending["a.send"] = wait_send_a
-        if STOP == "a_only":
-            return
 
         own = fbuf.at[y, xh]
         f_own = pltpu.make_async_copy(fin.at[k], own, sem("f_own"))
@@ -166,35 +186,37 @@
 
         lax.fori_loop(0, 16, invert, 0)
         need("a")
-        if STOP == "a":
-            return
-
-        b_dst = pbuf.at[:, z // 4, y, pl.ds(pl.multiple_of(8 * (z % 4), 8), 8), :]
-
-        def send_b_to(j, carry):
-            zd = (z + j) % 8
+
+        def b_place(zi):
+            return pbuf.at[:, zi // 4, y, pl.ds(pl.multiple_of(8 * (zi % 4), 8), 8), :]
+
+        def choose(zd):
             send_b[zd, 0] = buf_a[inv[2 * zd]]
             send_b[zd, 1] = buf_a[inv[2 * zd + 1]]
-            remote(send_b.at[zd], b_dst, sem("b.send"), sem("b"), r, col(zd, xl, k)).start()
-            return carry
-
-        lax.fori_loop(1, 8, send_b_to, 0)
-        send_b[z, 0] = buf_a[inv[2 * z]]
-        send_b[z, 1] = buf_a[inv[2 * z + 1]]
-        pltpu.make_async_copy(send_b.at[z], b_dst, sem("b")).start()
-        expect("b", pbuf.at[:, :, y])
+
+        def send_b_to(j, carry):
+            d = near_first(j)
+            zd = (z + d) % 8
+            choose(zd)
+            remote(send_b.at[zd], b_place(z), sem("b.send"), b_sems.at[d], r, col(zd, xl, k)).start()
+            return carry
+
+        choose(z)
+        pltpu.make_async_copy(send_b.at[z], b_place(z), b_sems.at[0]).start()
+        lax.fori_loop(0, 7, send_b_to, 0)
         expect("b.send", send_b.at[pl.ds(0, 7)])
+
         need("f_own", "f1", "f2", "f3")
         send("f_x", fbuf.at[:, xh], fbuf.at[:, xh], 2 * y + 1 - xh, col(z, 1 - xl, k), fbuf.at[:, 1 - xh])
-        if STOP == "f_x1":
-            return
-        need("b")
-        if STOP == "b":
-            return
-
-        mine = pbuf.at[:, :, y]
-        for d in (2, 1, 3):
-            send("c%d" % d, mine, mine, 2 * ((y + d) % 4) + xh, c, pbuf.at[:, :, (y + 4 - d) % 4])
+
+        for d in (0, 1, 7, 2, 6, 3, 5, 4):
+            place = b_place((z + 8 - d) % 8)
+            pltpu.make_async_copy(place, place, b_sems.at[d]).wait()
+            for dy in (2, 1, 3):
+                remote(place, place, sem("c.send"), sem("c"), 2 * ((y + dy) % 4) + xh, c).start()
+        three = pbuf.at[:, :, pl.ds(0, 3)]
+        expect("c", three)
+        expect("c.send", three)
         for t in range(2):
             start_either(
                 pbuf.at[t, xh, y], pdiag.at[xl], sem("pd%d.send" % t), sem("pd"),
@@ -210,23 +232,17 @@
         expect("pd", pdiag)
 
         need("anc")
-        if STOP == "anc":
-            return
         for j in range(4):
             high, low = halves(abuf[j])
             a_high[:, 128 * j : 128 * j + 128] = high
             a_low[:, 128 * j : 128 * j + 128] = low
 
-        need("c1", "c2", "c3")
-        if STOP == "c2":
-            return
+        need("c")
         p_high, p_low = halves(pbuf[...].reshape(512, 256))
         cbuf[...] = dot3(a_high[...], a_low[...], p_high, p_low).reshape(16, 32, 256)
-        if STOP == "product":
-            return
 
         def send_sum(j, carry):
-            zd, xd = (z + (j + 2) // 2) % 8, (xl + j) % 2
+            zd, xd = (z + far_first(j // 2)) % 8, (xl + 1 + j) % 2
             remote(
                 cbuf.at[2 * zd + xd], rbuf.at[xl, z], sem("sum.send"), sem("sum"), r, col(zd, xd, k)
             ).start()
@@ -242,27 +258,18 @@
         high, low = halves(fbuf[...].reshape(512, 512))
         f_high[...] = high
         f_low[...] = low
-        if STOP == "f_x":
-            return
         need("pd")
-        s_high, s_low = halves(jnp.concatenate([pdiag[0], pdiag[1]], axis=1))
-        spread[...] = dot3(s_high, s_low, f_high[...], f_low[...])
+        spread[...] = times_factor(jnp.concatenate([pdiag[0], pdiag[1]], axis=1), f_high, f_low)
         own_factor = fbuf[y, xh]
         own_sq[...] = jnp.sum(own_factor * own_factor, axis=0, keepdims=True)
-        if STOP == "spread":
-            return
         need("sum")
-        if STOP == "sum":
-            return
-
-        y_high, y_low = halves(jnp.concatenate([jnp.sum(rbuf[0], axis=0), jnp.sum(rbuf[1], axis=0)], axis=1))
-        result = dot3(y_high, y_low, f_high[...], f_low[...])
+
+        total = jnp.concatenate([jnp.sum(rbuf[0], axis=0), jnp.sum(rbuf[1], axis=0)], axis=1)
+        result = times_factor(total, f_high, f_low)
         prod[...] = -result.reshape(2, 16, 512)
         send("o", prod.at[1 - k], out_block.at[k], r, col(z, xl, 1 - k), out_block.at[1 - k])
         d_send[...] = jnp.sum(spread[...] * result, axis=0, keepdims=True)
         d1[q] = d_send[...]
-        if STOP == "apply":
-            return
 
         def send_d1(j, carry):
             remote(d_send, d1.at[q], sem("d1.send"), sem("d1"), r, (c + 2 * j) % 32).start()
@@ -274,8 +281,6 @@
         expect("d1.send", some)
         out_block[k] = prod[k]
         need("d1")
-        if STOP == "d1":
-            return
         d1_sum[...] = jnp.sum(d1[...], axis=0) + own_sq[...]
         d2[k, r] = d1_sum[...]
 
@@ -298,7 +303,7 @@
 
 def per_device(ancestor, panel, factor_inv, pattern):
     vmem = pltpu.VMEM
-    return pl.pallas_call(
+    block, diag = pl.pallas_call(
         kernel,
         out_shape=(jax.ShapeDtypeStruct((2, 16, 512), F32), jax.ShapeDtypeStruct((2, 512), F32)),
         in_specs=[pl.BlockSpec(memory_space=pl.ANY)] * 4,
@@ -325,12 +330,14 @@
             vmem((512, 512), BF16),
             vmem((512, 512), BF16),
             vmem((512, 512), BF16),
-            pltpu.SemaphoreType.DMA((80,)),
+            pltpu.SemaphoreType.DMA((48,)),
+            pltpu.SemaphoreType.DMA((8,)),
         ],
         compiler_params=pltpu.CompilerParams(
             collective_id=0, has_side_effects=True, vmem_limit_bytes=60 * 1024 * 1024
         ),
     )(ancestor, panel, factor_inv, pattern)
+    return block, diag
 
 
 def solution(mesh):

time: 63.6 us -> 57.7 us (0.907)
  Pallas kernels: 60.8 us -> 54.8 us
    pallas_call x1, Pallas kernels: 60.8 us -> 54.8 us  [per_device(): pl.pallas_call(kernel, out_shape=(jax.ShapeDtypeStruct((2, 16, 512), F32)...]
where the time goes in v3:
time: 57.7 us; the launch traced here: 57.5 us
  Pallas kernels  54.8 us (95%)
  local copies, waits for them, and re-layouts  2.07 us (4%)
  between operations  0.65 us (1%)
    pallas_call x1, Pallas kernels, per_device(): pl.pallas_call(kernel, out_shape=(jax.ShapeDtypeStruct((2, 16, 512), F32)...  54.8 us
    unnamed x4, local copies, waits for them, and re-layouts  2.07 us

profile of v3, /device:TPU:1, one launch (start us, length us, event | category | flops | bytes accessed | tf_op | source)
XLA Modules:
  0.0 57.5 jit_solution(16083542527723656547)
XLA Ops:
  0.6 54.8 %shard_map.59 = (f32[2,16,512]{2,1,0:T(8,128)}, f32[2,512]{1,0:T(2,128)}) custom-call(f32[2,512,128]{2,1,0:T(8,128)} %anc.1, f32[2,128,512]{2,1,0:T(8,128)} %pan.1, f32[2,64,512]{2,1,0:T(8,128)} %fin.1, s32[2,16]{1,0:T(2,128)} %pat_hbm.1), custom_call_target="tpu_custom_call" | custom-call | tf_op jit(solution)/shard_map/pallas_call | solution.py:306
  55.5 0.0 copy-start
  55.5 1.5 %copy.8 = f32[2,16,512]{2,1,0:T(8,128)} copy(f32[2,16,512]{2,1,0:T(8,128)} %get-tuple-element.4) | data formatting | bytes 131072
  57.0 0.0 copy-done
  57.0 0.6 %copy.9 = f32[2,512]{1,0:T(2,128)} copy(f32[2,512]{1,0:T(2,128)S(1)} %copy-done) | data formatting | bytes 8192
Async XLA Ops:
  55.5 1.5 %copy-start = (f32[2,512]{1,0:T(2,128)S(1)}, f32[2,512]{1,0:T(2,128)}, u32[]{:S(2)}) copy-start(f32[2,512]{1,0:T(2,128)} %get-tuple-element.5) | copy-start | bytes 12292

commit v4 on v3

--- a/solution.py
+++ b/solution.py
@@ -39,8 +39,8 @@
 
 def kernel(
     anc, pan, fin, pat_hbm, out_block, out_diag,
-    pat, inv, buf_a, send_b, pbuf, abuf, fbuf, cbuf, rbuf, pdiag, spread, prod, d_send, own_sq, d1, d1_sum, d2,
-    a_high, a_low, f_high, f_low, sems, b_sems,
+    pat, inv, buf_a, send_b, pbuf, abuf, fbuf, cbuf, rbuf, relay3, relay4, pdiag, spread, prod, d_send, own_sq, d1, d1_sum, d2,
+    a_high, a_low, f_high, f_low, sems, b_sems, relay_sems,
 ):
     r = lax.axis_index("row")
     c = lax.axis_index("col")
@@ -86,10 +86,6 @@
         @pl.when(jnp.logical_not(mine))
         def _():
             remote(src, dst, send_sem, recv_sem, row_, col_).start()
-
-    def far_first(j):
-        half = (j + 1) // 2
-        return 4 + jnp.where(j % 2 == 1, -half, half)
 
     def near_first(j):
         half = j // 2 + 1
@@ -241,19 +237,38 @@
         p_high, p_low = halves(pbuf[...].reshape(512, 256))
         cbuf[...] = dot3(a_high[...], a_low[...], p_high, p_low).reshape(16, 32, 256)
 
-        def send_sum(j, carry):
-            zd, xd = (z + far_first(j // 2)) % 8, (xl + 1 + j) % 2
-            remote(
-                cbuf.at[2 * zd + xd], rbuf.at[xl, z], sem("sum.send"), sem("sum"), r, col(zd, xd, k)
-            ).start()
-            return carry
-
-        lax.fori_loop(0, 14, send_sum, 0)
-        remote(cbuf.at[2 * z + 1 - xl], rbuf.at[xl, z], sem("sum.send"), sem("sum"), r, col(z, 1 - xl, k)).start()
-        all_but_own = cbuf.at[pl.ds(0, 15)]
-        expect("sum", all_but_own)
-        expect("sum.send", all_but_own)
-        rbuf[xl, z] = cbuf[q]
+        ways = ((1, pl.ds(0, 128)), (7, pl.ds(128, 128)))
+        xs = ((xl + 1) % 2, xl)
+        for i, xd in enumerate(xs):
+            for w, (up, half) in enumerate(ways):
+                remote(
+                    cbuf.at[2 * ((z + 4) % 8) + xd, :, half], relay4.at[w, i],
+                    sem("relay.send"), relay_sems.at[w, i, 0], r, col((z + 2 * up) % 8, xl, k),
+                ).start()
+                remote(
+                    cbuf.at[2 * ((z + 3 * up) % 8) + xd], relay3.at[w, i],
+                    sem("relay.send"), relay_sems.at[w, i, 1], r, col((z + up) % 8, xl, k),
+                ).start()
+
+        def send_sum(zd, xd, slot):
+            remote(cbuf.at[2 * zd + xd], rbuf.at[xl, slot], sem("sum.send"), sem("sum"), r, col(zd, xd, k)).start()
+
+        for xd in xs:
+            for w, (up, half) in enumerate(ways):
+                send_sum((z + up) % 8, xd, 1 + w)
+        send_sum(z, 1 - xl, 0)
+        rbuf[xl, 0] = cbuf[q]
+        expect("relay.send", cbuf.at[pl.ds(0, 6)])
+        expect("sum", cbuf.at[pl.ds(0, 9)])
+        expect("sum.send", cbuf.at[pl.ds(0, 9)])
+        for i, xd in enumerate(xs):
+            for w, (up, half) in enumerate(ways):
+                pltpu.make_async_copy(relay4.at[w, i], relay4.at[w, i], relay_sems.at[w, i, 0]).wait()
+                pltpu.make_async_copy(relay3.at[w, i], relay3.at[w, i], relay_sems.at[w, i, 1]).wait()
+                zd = (z + 2 * up) % 8
+                cbuf[2 * zd + xd] += relay3[w, i]
+                cbuf[2 * zd + xd, :, half] += relay4[w, i]
+                send_sum(zd, xd, 3 + w)
         need("f_x")
         high, low = halves(fbuf[...].reshape(512, 512))
         f_high[...] = high
@@ -317,7 +332,9 @@
             vmem((4, 512, 128), F32),
             vmem((4, 2, 64, 512), F32),
             vmem((16, 32, 256), F32),
-            vmem((2, 8, 32, 256), F32),
+            vmem((2, 5, 32, 256), F32),
+            vmem((2, 2, 32, 256), F32),
+            vmem((2, 2, 32, 128), F32),
             vmem((2, 32, 256), F32),
             vmem((32, 512), F32),
             vmem((2, 16, 512), F32),
@@ -332,11 +349,12 @@
             vmem((512, 512), BF16),
             pltpu.SemaphoreType.DMA((48,)),
             pltpu.SemaphoreType.DMA((8,)),
+            pltpu.SemaphoreType.DMA((2, 2, 2)),
         ],
         compiler_params=pltpu.CompilerParams(
-            collective_id=0, has_side_effects=True, vmem_limit_bytes=60 * 1024 * 1024
+            collective_id=0, has_side_effects=True, vmem_limit_bytes=32 * 1024 * 1024
         ),
-    )(ancestor, panel, factor_inv, pattern)
+    )(*[pltpu.with_memory_space_constraint(x, pltpu.HBM) for x in (ancestor, panel, factor_inv, pattern)])
     return block, diag
 
 

time: 57.7 us -> 53.8 us (0.932)
  Pallas kernels: 54.8 us -> 51.8 us
  local copies, waits for them, and re-layouts: 2.07 us -> 1.22 us
    pallas_call x1, Pallas kernels: 54.8 us -> 51.8 us  [per_device(): pl.pallas_call(kernel, out_shape=(jax.ShapeDtypeStruct((2, 16, 512), F32)...]
    unnamed x4 -> x2, local copies, waits for them, and re-layouts: 2.07 us -> 1.22 us
where the time goes in v4:
time: 53.8 us; the launch traced here: 53.7 us
  Pallas kernels  51.8 us (96%)
  local copies, waits for them, and re-layouts  1.22 us (2%)
  between operations  0.64 us (1%)
    pallas_call x1, Pallas kernels, per_device(): pl.pallas_call(kernel, out_shape=(jax.ShapeDtypeStruct((2, 16, 512), F32)...  51.8 us
    unnamed x2, local copies, waits for them, and re-layouts  1.22 us

profile of v4, /device:TPU:1, one launch (start us, length us, event | category | flops | bytes accessed | tf_op | source)
XLA Modules:
  0.0 53.7 jit_solution(6333161459553073445)
XLA Ops:
  0.6 51.8 %shard_map.59 = (f32[2,16,512]{2,1,0:T(8,128)S(1)}, f32[2,512]{1,0:T(2,128)S(1)}) custom-call(f32[2,512,128]{2,1,0:T(8,128)} %anc.1, f32[2,128,512]{2,1,0:T(8,128)} %pan.1, f32[2,64,512]{2,1,0:T(8,128)} %fin.1, s32[2,16]{1,0:T(2,128)} %pat_hbm.1), custom_call_target="tpu_custom_call" | custom-call | tf_op jit(solution)/shard_map/pallas_call | solution.py:321
  52.5 0.6 %copy.8 = f32[2,16,512]{2,1,0:T(8,128)} copy(f32[2,16,512]{2,1,0:T(8,128)S(1)} %get-tuple-element.4) | data formatting | bytes 131072
  53.1 0.6 %copy.9 = f32[2,512]{1,0:T(2,128)} copy(f32[2,512]{1,0:T(2,128)S(1)} %get-tuple-element.5) | data formatting | bytes 8192

commit v5 on v4

--- a/solution.py
+++ b/solution.py
@@ -39,7 +39,7 @@
 
 def kernel(
     anc, pan, fin, pat_hbm, out_block, out_diag,
-    pat, inv, buf_a, send_b, pbuf, abuf, fbuf, cbuf, rbuf, relay3, relay4, pdiag, spread, prod, d_send, own_sq, d1, d1_sum, d2,
+    pat, inv, buf_a, send_b, pbuf, abuf, fbuf, send_p, cbuf, rbuf, relay3, relay4, pdiag, spread, prod, d_send, own_sq, d1, d1_sum, d2,
     a_high, a_low, f_high, f_low, sems, b_sems, relay_sems,
 ):
     r = lax.axis_index("row")
@@ -114,21 +114,10 @@
 
         lax.fori_loop(1, 8, greet_row, 0)
         greet(2 * y + 1 - xh, col(z, 1 - xl, k))
-        pd_src_row = 2 * ((z % 2) * 2 + xl) + (z % 4) // 2
-        for x_src in range(2):
-            src_col = col(r, x_src, k)
-
-            @pl.when(jnp.logical_not(jnp.logical_and(pd_src_row == r, src_col == c)))
-            def _():
-                greet(pd_src_row, src_col)
-
-        others = 31 + 14 + 1
-        pd_mine = []
-        for t in range(2):
-            mine = jnp.logical_and(z == r, col(4 * t + 2 * xh + y // 2, y % 2, k) == c)
-            pd_mine.append(mine)
-            others = others + jnp.where(mine, jnp.int32(0), jnp.int32(1))
-        pl.semaphore_wait(barrier, others)
+        pl.semaphore_wait(barrier, 31 + 14 + 1)
+
+        pd_to, pd_x = 2 * (z // 4) + y // 2, y % 2
+        pd_self = jnp.logical_and(z % 4 == pd_to, xl == pd_x)
 
         def piece(zi, xi, s):
             return pan.at[
@@ -204,6 +193,38 @@
 
         need("f_own", "f1", "f2", "f3")
         send("f_x", fbuf.at[:, xh], fbuf.at[:, xh], 2 * y + 1 - xh, col(z, 1 - xl, k), fbuf.at[:, 1 - xh])
+
+        def send_pd(j, carry):
+            yd, t = (y + j // 2) % 4, j % 2
+            send_p[j] = buf_a[inv[2 * (2 * yd + xh) + t]]
+            place = pdiag.at[xl, pl.ds(pl.multiple_of(8 * (z % 4), 8), 8), :]
+            to_row, to_col = 2 * yd + xh, col(pd_to + 4 * t, pd_x, k)
+
+            def away():
+                remote(send_p.at[j], place, sem("pd.send"), sem("pd"), to_row, to_col).start()
+
+            if isinstance(j, int):
+                mine = to_col == c
+                pl.when(mine)(lambda: pltpu.make_async_copy(send_p.at[j], place, sem("pd")).start())
+                pl.when(jnp.logical_not(mine))(away)
+            else:
+                away()
+            return carry
+
+        lax.fori_loop(2, 8, send_pd, 0)
+        send_pd(0, 0)
+        send_pd(1, 0)
+        expect("pd", pdiag)
+
+        def wait_send_pd():
+            def wait_some(n):
+                some = send_p.at[pl.ds(0, n)]
+                pltpu.make_async_copy(some, some, sem("pd.send")).wait()
+
+            pl.when(pd_self)(lambda: wait_some(7))
+            pl.when(jnp.logical_not(pd_self))(lambda: wait_some(8))
+
+        pending["pd.send"] = wait_send_pd
 
         for d in (0, 1, 7, 2, 6, 3, 5, 4):
             place = b_place((z + 8 - d) % 8)
@@ -213,19 +234,6 @@
         three = pbuf.at[:, :, pl.ds(0, 3)]
         expect("c", three)
         expect("c.send", three)
-        for t in range(2):
-            start_either(
-                pbuf.at[t, xh, y], pdiag.at[xl], sem("pd%d.send" % t), sem("pd"),
-                z, col(4 * t + 2 * xh + y // 2, y % 2, k),
-            )
-
-            def wait_send_pd(t=t):
-                @pl.when(jnp.logical_not(pd_mine[t]))
-                def _():
-                    pltpu.make_async_copy(pdiag.at[0], pdiag.at[0], sem("pd%d.send" % t)).wait()
-
-            pending["pd%d.send" % t] = wait_send_pd
-        expect("pd", pdiag)
 
         need("anc")
         for j in range(4):
@@ -331,6 +339,7 @@
             vmem((2, 2, 4, 32, 256), F32),
             vmem((4, 512, 128), F32),
             vmem((4, 2, 64, 512), F32),
+            vmem((8, 8, 256), F32),
             vmem((16, 32, 256), F32),
             vmem((2, 5, 32, 256), F32),
             vmem((2, 2, 32, 256), F32),

time: 53.8 us -> 53.6 us (level)
  no operation moved by 1% of the time
where the time goes in v5:
time: 53.6 us
  Pallas kernels  51.7 us (96%)
  local copies, waits for them, and re-layouts  1.22 us (2%)
  between operations  0.64 us (1%)
    pallas_call x1, Pallas kernels, per_device(): pl.pallas_call(kernel, out_shape=(jax.ShapeDtypeStruct((2, 16, 512), F32)...  51.7 us
    unnamed x2, local copies, waits for them, and re-layouts  1.22 us

profile of v5, /device:TPU:1, one launch (start us, length us, event | category | flops | bytes accessed | tf_op | source)
XLA Modules:
  0.0 53.6 jit_solution(449330814048322109)
XLA Ops:
  0.6 51.7 %shard_map.59 = (f32[2,16,512]{2,1,0:T(8,128)S(1)}, f32[2,512]{1,0:T(2,128)S(1)}) custom-call(f32[2,512,128]{2,1,0:T(8,128)} %anc.1, f32[2,128,512]{2,1,0:T(8,128)} %pan.1, f32[2,64,512]{2,1,0:T(8,128)} %fin.1, s32[2,16]{1,0:T(2,128)} %pat_hbm.1), custom_call_target="tpu_custom_call" | custom-call | tf_op jit(solution)/shard_map/pallas_call | solution.py:329
  52.3 0.6 %copy.8 = f32[2,16,512]{2,1,0:T(8,128)} copy(f32[2,16,512]{2,1,0:T(8,128)S(1)} %get-tuple-element.4) | data formatting | bytes 131072
  53.0 0.6 %copy.9 = f32[2,512]{1,0:T(2,128)} copy(f32[2,512]{1,0:T(2,128)S(1)} %get-tuple-element.5) | data formatting | bytes 8192

commit v6 on v5

v6 whole, which is shorter than its diff:
```python
import jax
import jax.numpy as jnp
from jax import lax
from jax.experimental import pallas as pl
from jax.experimental.pallas import tpu as pltpu
from jax.sharding import PartitionSpec as P


MESH = pl.DeviceIdType.MESH
F32 = jnp.float32
BF16 = jnp.bfloat16


def halves(x):
    high = x.astype(BF16)
    low = (x - high.astype(F32)).astype(BF16)
    return high, low


def dot3(a_high, a_low, b_high, b_low):
    def dot(a, b):
        return jnp.dot(a, b, preferred_element_type=F32)

    return dot(a_high, b_high) + (dot(a_low, b_high) + dot(a_high, b_low))


def times_factor(x, f_high, f_low):
    high, low = halves(x)
    both = jnp.concatenate([high, low], axis=0)
    n = x.shape[0]

    def part(first, cols):
        rows = slice(first, 512)
        twice = jnp.dot(both[:, rows], f_high[rows, cols], preferred_element_type=F32)
        return twice[:n] + (twice[n:] + jnp.dot(high[:, rows], f_low[rows, cols], preferred_element_type=F32))

    return jnp.concatenate([part(0, slice(0, 256)), part(256, slice(256, 512))], axis=1)


def kernel(
    anc, pan, fin, pat_hbm, out_block, out_diag,
    pat, inv, buf_a, send_b, send_p, pbuf, abuf, fbuf, cbuf, rbuf, relay3, relay4, pdiag, spread, prod, d_send, own_sq,
    d1, d1_sum, d2, diag, a_high, a_low, f_high, f_low, sems, b_sems, relay_sems,
):
    r = lax.axis_index("row")
    c = lax.axis_index("col")
    y, xh = r // 2, r % 2
    z, xl, k = c // 4, (c // 2) % 2, c % 2
    q = 2 * z + xl

    names = {}
    pending = {}

    def sem(name):
        return sems.at[names.setdefault(name, len(names))]

    def col(z_, xl_, k_):
        return z_ * 4 + xl_ * 2 + k_

    def remote(src, dst, send_sem, recv_sem, row_, col_):
        return pltpu.make_async_remote_copy(
            src_ref=src, dst_ref=dst, send_sem=send_sem, recv_sem=recv_sem, device_id=(row_, col_), device_id_type=MESH
        )

    def wait_bytes(ref, s):
        pltpu.make_async_copy(ref, ref, s).wait()

    def expect(name, ref):
        pending[name] = lambda: wait_bytes(ref, sem(name))

    def need(*keys):
        for key in keys:
            pending.pop(key)()

    def send(name, src, dst, row_, col_, arrives):
        copy = remote(src, dst, sem(name + ".send"), sem(name), row_, col_)
        copy.start()
        pending[name + ".send"] = copy.wait_send
        if arrives is not None:
            expect(name, arrives)

    barrier = pltpu.get_barrier_semaphore()

    def greet(row_, col_):
        pl.semaphore_signal(barrier, inc=1, device_id=(row_, col_), device_id_type=MESH)

    def piece(zi, xi):
        return pan.at[:, pl.ds(pl.multiple_of(32 * y + 8 * (zi % 4), 8), 8), pl.ds(pl.multiple_of(256 * xi, 256), 256)]

    quarter = abuf.at[:, 2 * xl + k]

    @pl.when(k == 0)
    def _():
        greet(r, c + 1)
        pl.semaphore_wait(barrier, 16)

        def send_a(j, carry):
            zi, xi = (z + 3 - j // 2) % 4, (xl + j + 1) % 2
            remote(piece(zi, xi), buf_a.at[q], sem("a.send"), sem("a"), r, col(zi, xi, 1)).start()
            return carry

        lax.fori_loop(0, 8, send_a, 0)
        anc_x = remote(anc, quarter, sem("anc_x"), sem("anc"), r, col(z, 1 - xl, 1))
        anc_x.start()
        anc_core = remote(anc, quarter, sem("anc_core"), sem("anc"), r, c + 1)
        anc_core.start()
        wait_bytes(buf_a.at[pl.ds(0, 8)], sem("a.send"))
        anc_x.wait_send()
        anc_core.wait_send()
        wait_bytes(out_block, sem("o"))
        wait_bytes(out_diag, sem("diag"))

    def body():
        pat_copy = pltpu.make_async_copy(pat_hbm, pat, sem("pat"))
        pat_copy.start()
        pending["pat"] = pat_copy.wait

        def greet_col(j, carry):
            half = j // 2
            other = (c + 16 + jnp.where(j % 2 == 0, half, 32 - half)) % 32
            greet(r, other)
            return carry

        lax.fori_loop(1, 32, greet_col, 0)
        for d in (2, 1, 3):
            greet(2 * ((y + d) % 4) + xh, c)
        greet(2 * y + 1 - xh, col(z, 1 - xl, k))
        pl.semaphore_wait(barrier, 15 + 3 + 1 + 1)

        def send_a(j, carry):
            zi, xi = 4 + (z + j // 2) % 4, (xl + j) % 2
            remote(piece(zi, xi), buf_a.at[q], sem("a.send"), sem("a"), r, col(zi, xi, 1)).start()
            return carry

        lax.fori_loop(1, 8, send_a, 0)

        @pl.when(z >= 4)
        def _():
            pltpu.make_async_copy(piece(z, xl), buf_a.at[q], sem("a")).start()

        @pl.when(z < 4)
        def _():
            remote(piece(4 + z, xl), buf_a.at[q], sem("a.send"), sem("a"), r, col(4 + z, xl, 1)).start()

        expect("a", buf_a)

        def wait_send_a():
            pl.when(z >= 4)(lambda: wait_bytes(buf_a.at[pl.ds(0, 7)], sem("a.send")))
            pl.when(z < 4)(lambda: wait_bytes(buf_a.at[pl.ds(0, 8)], sem("a.send")))

        pending["a.send"] = wait_send_a

        own = fbuf.at[:, y, xh]
        f_own = pltpu.make_async_copy(fin, own, sem("f_own"))
        f_own.start()
        pending["f_own"] = f_own.wait
        for d in (2, 1, 3):
            send("f%d" % d, fin, own, 2 * ((y + d) % 4) + xh, c, fbuf.at[:, (y + 4 - d) % 4, xh])

        pltpu.make_async_copy(anc, quarter, sem("anc")).start()
        anc_x = remote(anc, quarter, sem("anc_x"), sem("anc"), r, col(z, 1 - xl, 1))
        anc_x.start()
        pending["anc_x"] = anc_x.wait_send
        expect("anc", abuf)

        need("pat")

        def invert(n, carry):
            for s in range(2):
                found = jnp.int32(0)
                for j in range(16):
                    found = jnp.where(pat[s, j] == n, jnp.int32(j), found)
                inv[s, n] = found
            return carry

        lax.fori_loop(0, 16, invert, 0)
        need("a")

        def b_place(zi):
            return pbuf.at[:, :, zi // 4, y, pl.ds(pl.multiple_of(8 * (zi % 4), 8), 8), :]

        def choose(zd):
            for s in range(2):
                for t in range(2):
                    send_b[zd, s, t] = buf_a[inv[s, 2 * zd + t], s]

        def near_first(j):
            half = j // 2 + 1
            return jnp.where(j % 2 == 0, half, 8 - half)

        def send_b_to(j, carry):
            d = near_first(j)
            zd = (z + d) % 8
            choose(zd)
            remote(send_b.at[zd], b_place(z), sem("b.send"), b_sems.at[d], r, col(zd, xl, k)).start()
            return carry

        choose(z)
        pltpu.make_async_copy(send_b.at[z], b_place(z), b_sems.at[0]).start()
        lax.fori_loop(0, 7, send_b_to, 0)
        expect("b.send", send_b.at[pl.ds(0, 7)])

        need("f_own", "f1", "f2", "f3")
        send("f_x", fbuf.at[:, :, xh], fbuf.at[:, :, xh], 2 * y + 1 - xh, col(z, 1 - xl, k), fbuf.at[:, :, 1 - xh])

        pd_to, pd_x = 2 * (z // 4) + y // 2, y % 2
        pd_self = jnp.logical_and(z % 4 == pd_to, xl == pd_x)

        def send_pd(j, carry):
            yd, t = (y + j // 2) % 4, j % 2
            for s in range(2):
                send_p[j, s] = buf_a[inv[s, 2 * (2 * yd + xh) + t], s]
            place = pdiag.at[:, xl, pl.ds(pl.multiple_of(8 * (z % 4), 8), 8), :]
            to_row, to_col = 2 * yd + xh, col(pd_to + 4 * t, pd_x, k)

            def away():
                remote(send_p.at[j], place, sem("pd.send"), sem("pd"), to_row, to_col).start()

            if isinstance(j, int):
                mine = to_col == c
                pl.when(mine)(lambda: pltpu.make_async_copy(send_p.at[j], place, sem("pd")).start())
                pl.when(jnp.logical_not(mine))(away)
            else:
                away()
            return carry

        lax.fori_loop(2, 8, send_pd, 0)
        send_pd(0, 0)
        send_pd(1, 0)
        expect("pd", pdiag)

        def wait_send_pd():
            pl.when(pd_self)(lambda: wait_bytes(send_p.at[pl.ds(0, 7)], sem("pd.send")))
            pl.when(jnp.logical_not(pd_self))(lambda: wait_bytes(send_p, sem("pd.send")))

        pending["pd.send"] = wait_send_pd

        for d in (0, 1, 7, 2, 6, 3, 5, 4):
            place = b_place((z + 8 - d) % 8)
            wait_bytes(place, b_sems.at[d])
            for dy in (2, 1, 3):
                remote(place, place, sem("c.send"), sem("c"), 2 * ((y + dy) % 4) + xh, c).start()
        three = pbuf.at[:, :, :, pl.ds(0, 3)]
        expect("c", three)
        expect("c.send", three)

        need("anc")
        for s in range(2):
            for j in range(4):
                high, low = halves(abuf[s, j])
                a_high[s, :, 128 * j : 128 * j + 128] = high
                a_low[s, :, 128 * j : 128 * j + 128] = low

        need("c")

        ways = ((1, pl.ds(0, 128)), (7, pl.ds(128, 128)))
        xs = ((xl + 1) % 2, xl)
        for s in range(2):
            p_high, p_low = halves(pbuf[s].reshape(512, 256))
            cbuf[s] = dot3(a_high[s], a_low[s], p_high, p_low).reshape(16, 32, 256)
            for i, xd in enumerate(xs):
                for w, (up, half) in enumerate(ways):
                    remote(
                        cbuf.at[s, 2 * ((z + 4) % 8) + xd, :, half], relay4.at[w, i, s],
                        sem("relay.send"), relay_sems.at[w, i, 0], r, col((z + 2 * up) % 8, xl, k),
                    ).start()
                    remote(
                        cbuf.at[s, 2 * ((z + 3 * up) % 8) + xd], relay3.at[w, i, s],
                        sem("relay.send"), relay_sems.at[w, i, 1], r, col((z + up) % 8, xl, k),
                    ).start()
        expect("relay.send", cbuf.at[:, pl.ds(0, 6)])

        def send_sum(zd, xd, slot):
            remote(
                cbuf.at[:, 2 * zd + xd], rbuf.at[xl, slot], sem("sum.send"), sem("sum"), r, col(zd, xd, k)
            ).start()

        for xd in xs:
            for w, (up, half) in enumerate(ways):
                send_sum((z + up) % 8, xd, 1 + w)
        send_sum(z, 1 - xl, 0)
        rbuf[xl, 0] = cbuf[:, q]
        expect("sum", cbuf.at[:, pl.ds(0, 9)])
        expect("sum.send", cbuf.at[:, pl.ds(0, 9)])

        for i, xd in enumerate(xs):
            for w, (up, half) in enumerate(ways):
                wait_bytes(relay4.at[w, i], relay_sems.at[w, i, 0])
                wait_bytes(relay3.at[w, i], relay_sems.at[w, i, 1])
                zd = (z + 2 * up) % 8
                for s in range(2):
                    cbuf[s, 2 * zd + xd] += relay3[w, i, s]
                    cbuf[s, 2 * zd + xd, :, half] += relay4[w, i, s]
                send_sum(zd, xd, 3 + w)

        need("f_x")
        own_rows = fbuf[:, y, xh]
        own_sq[...] = jnp.sum(own_rows * own_rows, axis=1)
        need("pd")
        for s in range(2):
            high, low = halves(fbuf[s].reshape(512, 512))
            f_high[s] = high
            f_low[s] = low
            spread[s] = times_factor(
                jnp.concatenate([pdiag[s, 0], pdiag[s, 1]], axis=1), f_high.at[s], f_low.at[s]
            )
        need("sum")

        for s in range(2):
            total = jnp.concatenate([jnp.sum(rbuf[0, :, s], axis=0), jnp.sum(rbuf[1, :, s], axis=0)], axis=1)
            result = times_factor(total, f_high.at[s], f_low.at[s])
            d_send[s : s + 1, :] = jnp.sum(spread[s] * result, axis=0, keepdims=True)
            prod[:, s] = -result.reshape(2, 16, 512)

        for dz in (4, 3, 5, 2, 6, 1, 7, 0):
            for xd in (1 - xl, xl):
                if dz or xd is not xl:
                    remote(d_send, d1.at[q], sem("d1.send"), sem("d1"), r, col((z + dz) % 8, xd, k)).start()
        expect("d1", d1.at[pl.ds(0, 15)])
        expect("d1.send", d1.at[pl.ds(0, 15)])
        d1[q] = d_send[...]
        send("o", prod.at[0], out_block, r, c - 1, None)
        out_block[...] = prod[1]
        need("d1")
        d1_sum[...] = jnp.sum(d1[...], axis=0) + own_sq[...]
        for dy, flip in ((2, 1), (1, 1), (3, 1), (2, 0), (0, 1), (1, 0), (3, 0)):
            to = 2 * ((y + dy) % 4) + (xh + flip) % 2
            remote(d1_sum, d2.at[r], sem("d2.send"), sem("d2"), to, c).start()
        d2[r] = d1_sum[...]
        expect("d2", d1.at[pl.ds(0, 7)])
        expect("d2.send", d1.at[pl.ds(0, 7)])
        need("d2")
        diag[...] = jnp.sum(d2[...], axis=0)
        send("diag", diag, out_diag, r, c - 1, None)
        out_diag[...] = diag[...]

    @pl.when(k == 1)
    def _():
        body()
        need(*pending)


def per_device(ancestor, panel, factor_inv, pattern):
    vmem = pltpu.VMEM
    inputs = [pltpu.with_memory_space_constraint(x, pltpu.HBM) for x in (ancestor, panel, factor_inv, pattern)]
    return pl.pallas_call(
        kernel,
        out_shape=(jax.ShapeDtypeStruct((2, 16, 512), F32), jax.ShapeDtypeStruct((2, 512), F32)),
        in_specs=[pl.BlockSpec(memory_space=pl.ANY)] * 4,
        out_specs=(pl.BlockSpec(memory_space=vmem), pl.BlockSpec(memory_space=vmem)),
        scratch_shapes=[
            pltpu.SMEM((2, 16), jnp.int32),
            pltpu.SMEM((2, 16), jnp.int32),
            vmem((16, 2, 8, 256), F32),
            vmem((8, 2, 2, 8, 256), F32),
            vmem((8, 2, 8, 256), F32),
            vmem((2, 2, 2, 4, 32, 256), F32),
            vmem((2, 4, 512, 128), F32),
            vmem((2, 4, 2, 64, 512), F32),
            vmem((2, 16, 32, 256), F32),
            vmem((2, 5, 2, 32, 256), F32),
            vmem((2, 2, 2, 32, 256), F32),
            vmem((2, 2, 2, 32, 128), F32),
            vmem((2, 2, 32, 256), F32),
            vmem((2, 32, 512), F32),
            vmem((2, 2, 16, 512), F32),
            vmem((2, 512), F32),
            vmem((2, 512), F32),
            vmem((16, 2, 512), F32),
            vmem((2, 512), F32),
            vmem((8, 2, 512), F32),
            vmem((2, 512), F32),
            vmem((2, 512, 512), BF16),
            vmem((2, 512, 512), BF16),
            vmem((2, 512, 512), BF16),
            vmem((2, 512, 512), BF16),
            pltpu.SemaphoreType.DMA((40,)),
            pltpu.SemaphoreType.DMA((8,)),
            pltpu.SemaphoreType.DMA((2, 2, 2)),
        ],
        compiler_params=pltpu.CompilerParams(
            collective_id=0, has_side_effects=True, vmem_limit_bytes=32 * 1024 * 1024
        ),
    )(*inputs)


def solution(mesh):
    in_specs = (P(None, "row", "col"), P(None, "col", None), P(None, "row", None), P())
    out_specs = (P(None, ("row", "col"), None), P())
    return jax.shard_map(per_device, mesh=mesh, in_specs=in_specs, out_specs=out_specs, check_vma=False)
```

time: 53.6 us -> 52.1 us (0.972)
  Pallas kernels: 51.7 us -> 50.2 us
    pallas_call x1, Pallas kernels: 51.7 us -> 50.2 us  [per_device(): pl.pallas_call(kernel, out_shape=(jax.ShapeDtypeStruct((2, 16, 512), F32)...]
where the time goes in v6:
time: 52.1 us; the launch traced here: 52 us
  Pallas kernels  50.2 us (96%)
  local copies, waits for them, and re-layouts  1.22 us (2%)
  between operations  0.64 us (1%)
    pallas_call x1, Pallas kernels, per_device(): pl.pallas_call(kernel, out_shape=(jax.ShapeDtypeStruct((2, 16, 512), F32)...  50.2 us
    unnamed x2, local copies, waits for them, and re-layouts  1.22 us

profile of v6, /device:TPU:1, one launch (start us, length us, event | category | flops | bytes accessed | tf_op | source)
XLA Modules:
  0.0 52.0 jit_solution(17174795805773576190)
XLA Ops:
  0.6 50.2 %shard_map.59 = (f32[2,16,512]{2,1,0:T(8,128)S(1)}, f32[2,512]{1,0:T(2,128)S(1)}) custom-call(f32[2,512,128]{2,1,0:T(8,128)} %anc.1, f32[2,128,512]{2,1,0:T(8,128)} %pan.1, f32[2,64,512]{2,1,0:T(8,128)} %fin.1, s32[2,16]{1,0:T(2,128)} %pat_hbm.1), custom_call_target="tpu_custom_call" | custom-call | tf_op jit(solution)/shard_map/pallas_call | solution.py:346
  50.8 0.6 %copy.8 = f32[2,16,512]{2,1,0:T(8,128)} copy(f32[2,16,512]{2,1,0:T(8,128)S(1)} %get-tuple-element.4) | data formatting | bytes 131072
  51.4 0.6 %copy.9 = f32[2,512]{1,0:T(2,128)} copy(f32[2,512]{1,0:T(2,128)S(1)} %get-tuple-element.5) | data formatting | bytes 8192

commit v7 on v6

--- a/solution.py
+++ b/solution.py
@@ -85,7 +85,7 @@
         pl.semaphore_signal(barrier, inc=1, device_id=(row_, col_), device_id_type=MESH)
 
     def piece(zi, xi):
-        return pan.at[:, pl.ds(pl.multiple_of(32 * y + 8 * (zi % 4), 8), 8), pl.ds(pl.multiple_of(256 * xi, 256), 256)]
+        return pan.at[:, pl.ds(pl.multiple_of(32 * (zi % 4) + 8 * y, 8), 8), pl.ds(pl.multiple_of(256 * xi, 256), 256)]
 
     quarter = abuf.at[:, 2 * xl + k]
 
@@ -177,7 +177,7 @@
         need("a")
 
         def b_place(zi):
-            return pbuf.at[:, :, zi // 4, y, pl.ds(pl.multiple_of(8 * (zi % 4), 8), 8), :]
+            return pbuf.at[:, :, zi, y]
 
         def choose(zd):
             for s in range(2):
@@ -202,38 +202,6 @@
 
         need("f_own", "f1", "f2", "f3")
         send("f_x", fbuf.at[:, :, xh], fbuf.at[:, :, xh], 2 * y + 1 - xh, col(z, 1 - xl, k), fbuf.at[:, :, 1 - xh])
-
-        pd_to, pd_x = 2 * (z // 4) + y // 2, y % 2
-        pd_self = jnp.logical_and(z % 4 == pd_to, xl == pd_x)
-
-        def send_pd(j, carry):
-            yd, t = (y + j // 2) % 4, j % 2
-            for s in range(2):
-                send_p[j, s] = buf_a[inv[s, 2 * (2 * yd + xh) + t], s]
-            place = pdiag.at[:, xl, pl.ds(pl.multiple_of(8 * (z % 4), 8), 8), :]
-            to_row, to_col = 2 * yd + xh, col(pd_to + 4 * t, pd_x, k)
-
-            def away():
-                remote(send_p.at[j], place, sem("pd.send"), sem("pd"), to_row, to_col).start()
-
-            if isinstance(j, int):
-                mine = to_col == c
-                pl.when(mine)(lambda: pltpu.make_async_copy(send_p.at[j], place, sem("pd")).start())
-                pl.when(jnp.logical_not(mine))(away)
-            else:
-                away()
-            return carry
-
-        lax.fori_loop(2, 8, send_pd, 0)
-        send_pd(0, 0)
-        send_pd(1, 0)
-        expect("pd", pdiag)
-
-        def wait_send_pd():
-            pl.when(pd_self)(lambda: wait_bytes(send_p.at[pl.ds(0, 7)], sem("pd.send")))
-            pl.when(jnp.logical_not(pd_self))(lambda: wait_bytes(send_p, sem("pd.send")))
-
-        pending["pd.send"] = wait_send_pd
 
         for d in (0, 1, 7, 2, 6, 3, 5, 4):
             place = b_place((z + 8 - d) % 8)
@@ -243,6 +211,38 @@
         three = pbuf.at[:, :, :, pl.ds(0, 3)]
         expect("c", three)
         expect("c.send", three)
+        pd_to, pd_x = z // 2, z % 2
+        pd_self = jnp.logical_and(jnp.logical_or(pd_to == z, pd_to + 4 == z), xl == pd_x)
+
+        def send_pd(j, carry):
+            yd, t = (y + j // 2) % 4, j % 2
+            for s in range(2):
+                send_p[j, s] = buf_a[inv[s, 2 * (2 * yd + xh) + t], s]
+            place = pdiag.at[:, xl, pl.ds(pl.multiple_of(8 * y, 8), 8), :]
+            to_row, to_col = 2 * yd + xh, col(pd_to + 4 * t, pd_x, k)
+
+            def away():
+                remote(send_p.at[j], place, sem("pd.send"), sem("pd"), to_row, to_col).start()
+
+            if isinstance(j, int):
+                mine = to_col == c
+                pl.when(mine)(lambda: pltpu.make_async_copy(send_p.at[j], place, sem("pd")).start())
+                pl.when(jnp.logical_not(mine))(away)
+            else:
+                away()
+            return carry
+
+        lax.fori_loop(2, 8, send_pd, 0)
+        send_pd(0, 0)
+        send_pd(1, 0)
+        expect("pd", pdiag)
+
+        def wait_send_pd():
+            pl.when(pd_self)(lambda: wait_bytes(send_p.at[pl.ds(0, 7)], sem("pd.send")))
+            pl.when(jnp.logical_not(pd_self))(lambda: wait_bytes(send_p, sem("pd.send")))
+
+        pending["pd.send"] = wait_send_pd
+
 
         need("anc")
         for s in range(2):
@@ -354,7 +354,7 @@
             vmem((16, 2, 8, 256), F32),
             vmem((8, 2, 2, 8, 256), F32),
             vmem((8, 2, 8, 256), F32),
-            vmem((2, 2, 2, 4, 32, 256), F32),
+            vmem((2, 2, 8, 4, 8, 256), F32),
             vmem((2, 4, 512, 128), F32),
             vmem((2, 4, 2, 64, 512), F32),
             vmem((2, 16, 32, 256), F32),

time: 52.1 us -> 49.6 us (0.952)
  Pallas kernels: 50.2 us -> 47.7 us
    pallas_call x1, Pallas kernels: 50.2 us -> 47.7 us  [per_device(): pl.pallas_call(kernel, out_shape=(jax.ShapeDtypeStruct((2, 16, 512), F32)...]
where the time goes in v7:
time: 49.6 us; the launch traced here: 49.5 us
  Pallas kernels  47.7 us (96%)
  local copies, waits for them, and re-layouts  1.22 us (2%)
  between operations  0.64 us (1%)
    pallas_call x1, Pallas kernels, per_device(): pl.pallas_call(kernel, out_shape=(jax.ShapeDtypeStruct((2, 16, 512), F32)...  47.7 us
    unnamed x2, local copies, waits for them, and re-layouts  1.22 us

profile of v7, /device:TPU:1, one launch (start us, length us, event | category | flops | bytes accessed | tf_op | source)
XLA Modules:
  0.0 49.5 jit_solution(898445624833407906)
XLA Ops:
  0.6 47.7 %shard_map.59 = (f32[2,16,512]{2,1,0:T(8,128)S(1)}, f32[2,512]{1,0:T(2,128)S(1)}) custom-call(f32[2,512,128]{2,1,0:T(8,128)} %anc.1, f32[2,128,512]{2,1,0:T(8,128)} %pan.1, f32[2,64,512]{2,1,0:T(8,128)} %fin.1, s32[2,16]{1,0:T(2,128)} %pat_hbm.1), custom_call_target="tpu_custom_call" | custom-call | tf_op jit(solution)/shard_map/pallas_call | solution.py:346
  48.3 0.6 %copy.8 = f32[2,16,512]{2,1,0:T(8,128)} copy(f32[2,16,512]{2,1,0:T(8,128)S(1)} %get-tuple-element.4) | data formatting | bytes 131072
  48.9 0.6 %copy.9 = f32[2,512]{1,0:T(2,128)} copy(f32[2,512]{1,0:T(2,128)S(1)} %get-tuple-element.5) | data formatting | bytes 8192

commit v8 on v7

--- a/solution.py
+++ b/solution.py
@@ -40,7 +40,7 @@
 def kernel(
     anc, pan, fin, pat_hbm, out_block, out_diag,
     pat, inv, buf_a, send_b, send_p, pbuf, abuf, fbuf, cbuf, rbuf, relay3, relay4, pdiag, spread, prod, d_send, own_sq,
-    d1, d1_sum, d2, diag, a_high, a_low, f_high, f_low, sems, b_sems, relay_sems,
+    d1, d1_sum, d2, a_high, a_low, f_high, f_low, sems, b_sems, relay_sems,
 ):
     r = lax.axis_index("row")
     c = lax.axis_index("col")
@@ -91,7 +91,11 @@
 
     @pl.when(k == 0)
     def _():
-        greet(r, c + 1)
+        def greet_row(j, carry):
+            greet((r + j) % 8, c + 1)
+            return carry
+
+        lax.fori_loop(0, 8, greet_row, 0)
         pl.semaphore_wait(barrier, 16)
 
         def send_a(j, carry):
@@ -108,7 +112,8 @@
         anc_x.wait_send()
         anc_core.wait_send()
         wait_bytes(out_block, sem("o"))
-        wait_bytes(out_diag, sem("diag"))
+        wait_bytes(d2, sem("d2"))
+        out_diag[...] = jnp.sum(d2[...], axis=0)
 
     def body():
         pat_copy = pltpu.make_async_copy(pat_hbm, pat, sem("pat"))
@@ -125,7 +130,7 @@
         for d in (2, 1, 3):
             greet(2 * ((y + d) % 4) + xh, c)
         greet(2 * y + 1 - xh, col(z, 1 - xl, k))
-        pl.semaphore_wait(barrier, 15 + 3 + 1 + 1)
+        pl.semaphore_wait(barrier, 15 + 3 + 1 + 8)
 
         def send_a(j, carry):
             zi, xi = 4 + (z + j // 2) % 4, (xl + j) % 2
@@ -201,7 +206,12 @@
         expect("b.send", send_b.at[pl.ds(0, 7)])
 
         need("f_own", "f1", "f2", "f3")
-        send("f_x", fbuf.at[:, :, xh], fbuf.at[:, :, xh], 2 * y + 1 - xh, col(z, 1 - xl, k), fbuf.at[:, :, 1 - xh])
+        for y_ in range(4):
+            width = pl.ds(0, 128 * (y_ + 1))
+            send(
+                "f_x%d" % y_, fbuf.at[:, y_, xh, :, width], fbuf.at[:, y_, xh, :, width],
+                2 * y + 1 - xh, col(z, 1 - xl, k), fbuf.at[:, y_, 1 - xh, :, width],
+            )
 
         for d in (0, 1, 7, 2, 6, 3, 5, 4):
             place = b_place((z + 8 - d) % 8)
@@ -293,14 +303,19 @@
                     cbuf[s, 2 * zd + xd, :, half] += relay4[w, i, s]
                 send_sum(zd, xd, 3 + w)
 
-        need("f_x")
+        need("f_x0", "f_x1", "f_x2", "f_x3")
         own_rows = fbuf[:, y, xh]
         own_sq[...] = jnp.sum(own_rows * own_rows, axis=1)
         need("pd")
         for s in range(2):
-            high, low = halves(fbuf[s].reshape(512, 512))
-            f_high[s] = high
-            f_low[s] = low
+            for y_ in range(4):
+                rows, width = slice(128 * y_, 128 * y_ + 128), 128 * (y_ + 1)
+                high, low = halves(fbuf[s, y_, :, :, :width].reshape(128, width))
+                f_high[s, rows, :width] = high
+                f_low[s, rows, :width] = low
+                if y_ % 2 == 0:
+                    f_high[s, rows, width : width + 128] = jnp.zeros((128, 128), BF16)
+                    f_low[s, rows, width : width + 128] = jnp.zeros((128, 128), BF16)
             spread[s] = times_factor(
                 jnp.concatenate([pdiag[s, 0], pdiag[s, 1]], axis=1), f_high.at[s], f_low.at[s]
             )
@@ -323,16 +338,16 @@
         out_block[...] = prod[1]
         need("d1")
         d1_sum[...] = jnp.sum(d1[...], axis=0) + own_sq[...]
-        for dy, flip in ((2, 1), (1, 1), (3, 1), (2, 0), (0, 1), (1, 0), (3, 0)):
+        for dy, flip in ((2, 1), (1, 1), (3, 1), (2, 0), (0, 1), (1, 0), (3, 0), (0, 0)):
             to = 2 * ((y + dy) % 4) + (xh + flip) % 2
-            remote(d1_sum, d2.at[r], sem("d2.send"), sem("d2"), to, c).start()
+            remote(d1_sum, d2.at[r], sem("d2.send"), sem("d2"), to, c - 1).start()
+            if dy or flip:
+                remote(d1_sum, d2.at[r], sem("d2.send"), sem("d2"), to, c).start()
         d2[r] = d1_sum[...]
         expect("d2", d1.at[pl.ds(0, 7)])
-        expect("d2.send", d1.at[pl.ds(0, 7)])
+        expect("d2.send", d1.at[pl.ds(0, 15)])
         need("d2")
-        diag[...] = jnp.sum(d2[...], axis=0)
-        send("diag", diag, out_diag, r, c - 1, None)
-        out_diag[...] = diag[...]
+        out_diag[...] = jnp.sum(d2[...], axis=0)
 
     @pl.when(k == 1)
     def _():
@@ -369,7 +384,6 @@
             vmem((16, 2, 512), F32),
             vmem((2, 512), F32),
             vmem((8, 2, 512), F32),
-            vmem((2, 512), F32),
             vmem((2, 512, 512), BF16),
             vmem((2, 512, 512), BF16),
             vmem((2, 512, 512), BF16),

time: 49.6 us -> 49.1 us (0.990)
  Pallas kernels: 47.7 us -> 47.2 us
where the time goes in v8:
time: 49.1 us
  Pallas kernels  47.2 us (96%)
  local copies, waits for them, and re-layouts  1.22 us (2%)
  between operations  0.64 us (1%)
    pallas_call x1, Pallas kernels, per_device(): pl.pallas_call(kernel, out_shape=(jax.ShapeDtypeStruct((2, 16, 512), F32)...  47.2 us
    unnamed x2, local copies, waits for them, and re-layouts  1.22 us

profile of v8, /device:TPU:1, one launch (start us, length us, event | category | flops | bytes accessed | tf_op | source)
XLA Modules:
  0.0 49.1 jit_solution(12684069251536365086)
XLA Ops:
  0.6 47.2 %shard_map.59 = (f32[2,16,512]{2,1,0:T(8,128)S(1)}, f32[2,512]{1,0:T(2,128)S(1)}) custom-call(f32[2,512,128]{2,1,0:T(8,128)} %anc.1, f32[2,128,512]{2,1,0:T(8,128)} %pan.1, f32[2,64,512]{2,1,0:T(8,128)} %fin.1, s32[2,16]{1,0:T(2,128)} %pat_hbm.1), custom_call_target="tpu_custom_call" | custom-call | tf_op jit(solution)/shard_map/pallas_call | solution.py:361
  47.8 0.6 %copy.8 = f32[2,16,512]{2,1,0:T(8,128)} copy(f32[2,16,512]{2,1,0:T(8,128)S(1)} %get-tuple-element.4) | data formatting | bytes 131072
  48.5 0.6 %copy.9 = f32[2,512]{1,0:T(2,128)} copy(f32[2,512]{1,0:T(2,128)S(1)} %get-tuple-element.5) | data formatting | bytes 8192

commit v9 on v8

--- a/solution.py
+++ b/solution.py
@@ -40,7 +40,7 @@
 def kernel(
     anc, pan, fin, pat_hbm, out_block, out_diag,
     pat, inv, buf_a, send_b, send_p, pbuf, abuf, fbuf, cbuf, rbuf, relay3, relay4, pdiag, spread, prod, d_send, own_sq,
-    d1, d1_sum, d2, a_high, a_low, f_high, f_low, sems, b_sems, relay_sems,
+    d1, d1_sum, d2, a_high, a_low, p_high, p_low, f_high, f_low, sems, b_sems, relay_sems,
 ):
     r = lax.axis_index("row")
     c = lax.axis_index("col")
@@ -265,9 +265,19 @@
 
         ways = ((1, pl.ds(0, 128)), (7, pl.ds(128, 128)))
         xs = ((xl + 1) % 2, xl)
+        def product(s, places):
+            rows = [pl.ds(pl.multiple_of(64 * zd, 64), 64) for zd in places]
+            left_high = jnp.concatenate([a_high[s, some, :] for some in rows], axis=0)
+            left_low = jnp.concatenate([a_low[s, some, :] for some in rows], axis=0)
+            sums = dot3(left_high, left_low, p_high[s], p_low[s])
+            for n, zd in enumerate(places):
+                cbuf[s, pl.ds(2 * zd, 2)] = sums[64 * n : 64 * n + 64].reshape(2, 32, 256)
+
         for s in range(2):
-            p_high, p_low = halves(pbuf[s].reshape(512, 256))
-            cbuf[s] = dot3(a_high[s], a_low[s], p_high, p_low).reshape(16, 32, 256)
+            high, low = halves(pbuf[s].reshape(512, 256))
+            p_high[s] = high
+            p_low[s] = low
+            product(s, [(z + d) % 8 for d in (4, 3, 5)])
             for i, xd in enumerate(xs):
                 for w, (up, half) in enumerate(ways):
                     remote(
@@ -278,6 +288,8 @@
                         cbuf.at[s, 2 * ((z + 3 * up) % 8) + xd], relay3.at[w, i, s],
                         sem("relay.send"), relay_sems.at[w, i, 1], r, col((z + up) % 8, xl, k),
                     ).start()
+        for s in range(2):
+            product(s, [(z + d) % 8 for d in (1, 7, 2, 6, 0)])
         expect("relay.send", cbuf.at[:, pl.ds(0, 6)])
 
         def send_sum(zd, xd, slot):
@@ -386,6 +398,8 @@
             vmem((8, 2, 512), F32),
             vmem((2, 512, 512), BF16),
             vmem((2, 512, 512), BF16),
+            vmem((2, 512, 256), BF16),
+            vmem((2, 512, 256), BF16),
             vmem((2, 512, 512), BF16),
             vmem((2, 512, 512), BF16),
             pltpu.SemaphoreType.DMA((40,)),

time: 49.1 us -> 48.6 us (0.990)
  Pallas kernels: 47.2 us -> 46.7 us
    pallas_call x1, Pallas kernels: 47.2 us -> 46.7 us  [per_device(): pl.pallas_call(kernel, out_shape=(jax.ShapeDtypeStruct((2, 16, 512), F32)...]
where the time goes in v9:
time: 48.6 us
  Pallas kernels  46.7 us (96%)
  local copies, waits for them, and re-layouts  1.22 us (3%)
  between operations  0.64 us (1%)
    pallas_call x1, Pallas kernels, per_device(): pl.pallas_call(kernel, out_shape=(jax.ShapeDtypeStruct((2, 16, 512), F32)...  46.7 us
    unnamed x2, local copies, waits for them, and re-layouts  1.22 us

profile of v9, /device:TPU:1, one launch (start us, length us, event | category | flops | bytes accessed | tf_op | source)
XLA Modules:
  0.0 48.6 jit_solution(16094913562808810241)
XLA Ops:
  0.6 46.7 %shard_map.59 = (f32[2,16,512]{2,1,0:T(8,128)S(1)}, f32[2,512]{1,0:T(2,128)S(1)}) custom-call(f32[2,512,128]{2,1,0:T(8,128)} %anc.1, f32[2,128,512]{2,1,0:T(8,128)} %pan.1, f32[2,64,512]{2,1,0:T(8,128)} %fin.1, s32[2,16]{1,0:T(2,128)} %pat_hbm.1), custom_call_target="tpu_custom_call" | custom-call | tf_op jit(solution)/shard_map/pallas_call | solution.py:373
  47.3 0.6 %copy.8 = f32[2,16,512]{2,1,0:T(8,128)} copy(f32[2,16,512]{2,1,0:T(8,128)S(1)} %get-tuple-element.4) | data formatting | bytes 131072
  48.0 0.6 %copy.9 = f32[2,512]{1,0:T(2,128)} copy(f32[2,512]{1,0:T(2,128)S(1)} %get-tuple-element.5) | data formatting | bytes 8192

commit v10 on v9

--- a/solution.py
+++ b/solution.py
@@ -333,11 +333,12 @@
             )
         need("sum")
 
+        results = []
         for s in range(2):
             total = jnp.concatenate([jnp.sum(rbuf[0, :, s], axis=0), jnp.sum(rbuf[1, :, s], axis=0)], axis=1)
             result = times_factor(total, f_high.at[s], f_low.at[s])
             d_send[s : s + 1, :] = jnp.sum(spread[s] * result, axis=0, keepdims=True)
-            prod[:, s] = -result.reshape(2, 16, 512)
+            results.append(result)
 
         for dz in (4, 3, 5, 2, 6, 1, 7, 0):
             for xd in (1 - xl, xl):
@@ -346,6 +347,8 @@
         expect("d1", d1.at[pl.ds(0, 15)])
         expect("d1.send", d1.at[pl.ds(0, 15)])
         d1[q] = d_send[...]
+        for s in range(2):
+            prod[:, s] = -results[s].reshape(2, 16, 512)
         send("o", prod.at[0], out_block, r, c - 1, None)
         out_block[...] = prod[1]
         need("d1")

time: 48.6 us -> 48.6 us (level)
  no operation moved by 1% of the time
where the time goes in v10:
time: 48.6 us
  Pallas kernels  46.7 us (96%)
  local copies, waits for them, and re-layouts  1.22 us (3%)
  between operations  0.64 us (1%)
    pallas_call x1, Pallas kernels, per_device(): pl.pallas_call(kernel, out_shape=(jax.ShapeDtypeStruct((2, 16, 512), F32)...  46.7 us
    unnamed x2, local copies, waits for them, and re-layouts  1.22 us

profile of v10, /device:TPU:1, one launch (start us, length us, event | category | flops | bytes accessed | tf_op | source)
XLA Modules:
  0.0 48.6 jit_solution(11410221867198243507)
XLA Ops:
  0.6 46.7 %shard_map.59 = (f32[2,16,512]{2,1,0:T(8,128)S(1)}, f32[2,512]{1,0:T(2,128)S(1)}) custom-call(f32[2,512,128]{2,1,0:T(8,128)} %anc.1, f32[2,128,512]{2,1,0:T(8,128)} %pan.1, f32[2,64,512]{2,1,0:T(8,128)} %fin.1, s32[2,16]{1,0:T(2,128)} %pat_hbm.1), custom_call_target="tpu_custom_call" | custom-call | tf_op jit(solution)/shard_map/pallas_call | solution.py:376
  47.3 0.6 %copy.8 = f32[2,16,512]{2,1,0:T(8,128)} copy(f32[2,16,512]{2,1,0:T(8,128)S(1)} %get-tuple-element.4) | data formatting | bytes 131072
  48.0 0.6 %copy.9 = f32[2,512]{1,0:T(2,128)} copy(f32[2,512]{1,0:T(2,128)S(1)} %get-tuple-element.5) | data formatting | bytes 8192
